TPU v7x, 256 devices: a whole 4x4x8 slice. The times are simulated.
256 devices in a mesh: fin: 16 (over y, z_lo), fout: 16 (over x, z_hi, core).
Axes of the slice: x: 4, y: 4, z: 8 (z_hi: 2, z_lo: 4; z = z_hi * 4 + z_lo), core: 2. Of those that a mesh axis runs over, the one named last changes fastest.
Arguments:
- tokens: bfloat16 [256, 6144], P(None, 'fin'), may hold values from -60 to 60
- norm_gain: float32 [6144], P('fin'), may hold values from 0.1 to 1.9
- attend_weight: bfloat16 [3, 6144, 6144], P(None, 'fin', 'fout'), may hold values from -0.078125 to 0.078125
- up_weight: bfloat16 [6144, 24576], P('fin', 'fout'), may hold values from -0.078125 to 0.078125
- out_weight: bfloat16 [6144, 6144], P('fout', 'fin'), may hold values from -0.078125 to 0.078125
- down_weight: bfloat16 [24576, 6144], P('fout', 'fin'), may hold values from -0.0390625 to 0.0390625
- upstream: bfloat16 [256, 6144], P(None, 'fin'), may hold values from -6 to 6
Outputs:
- layer_out: bfloat16 [256, 6144], P(None, 'fin')
- tokens_grad: bfloat16 [256, 6144], P(None, 'fin')
- gain_grad: float32 [6144], P('fin')
- attend_grad: bfloat16 [3, 6144, 6144], P(None, 'fin', 'fout')
- up_grad: bfloat16 [6144, 24576], P('fin', 'fout')
- out_grad: bfloat16 [6144, 6144], P('fout', 'fin')
- down_grad: bfloat16 [24576, 6144], P('fout', 'fin')
All inputs are finite; a program needn't handle non-finite values.
Results may differ from a plain program's by a relative error of at most 0.024.
Values may be sent and summed in bfloat16 or wider, within the bound.
A program may use at most 64 MiB of HBM per device.

v0:
```python
import jax
import jax.numpy as jnp
from jax import lax
from jax.sharding import PartitionSpec as P

D = 6144
HEAD_DIM = 128
SEQ = 256


EPS = 1e-06


def left_contract(left, right):
    return lax.dot_general(
        left, right, (((0,), (0,)), ((), ())), preferred_element_type=jnp.float32
    )


def right_contract(left, right):
    return lax.dot_general(
        left, right, (((1,), (1,)), ((), ())), preferred_element_type=jnp.float32
    )


def head_norm(values, local_heads):
    count = values.shape[0]
    split = values.reshape(count, local_heads, HEAD_DIM)
    centred = split - jnp.mean(split, -1, keepdims=True)
    scales = lax.rsqrt(jnp.mean(centred * centred, -1, keepdims=True) + EPS)
    return ((centred * scales).reshape(count, -1), scales)


def norm_back(grads, normed, scales, local_heads):
    count = grads.shape[0]
    upper = grads.reshape(count, local_heads, HEAD_DIM)
    shaped = normed.reshape(count, local_heads, HEAD_DIM)
    inner = (
        upper
        - jnp.mean(upper, -1, keepdims=True)
        - shaped * jnp.mean(upper * shaped, -1, keepdims=True)
    )
    return (scales * inner).reshape(count, -1)


def gelu_value(values):
    return 0.5 * values * (1.0 + jax.scipy.special.erf(values * 0.7071067811865476))


def gelu_slope(values):
    return (
        0.5 * (1.0 + jax.scipy.special.erf(values * 0.7071067811865476))
        + values * jnp.exp(-0.5 * values * values) * 0.3989422804014327
    )


def make_terms(normed_rows, members):
    return jnp.concatenate(
        [jnp.dot(normed_rows, member, preferred_element_type=jnp.float32) for member in members], 1
    )


def make_fold(normed_rows, members, shard_rows):
    amount = shard_rows.shape[0]
    weight_acc = left_contract(normed_rows, shard_rows)
    cursor = 0
    product_sum = jnp.zeros((amount, normed_rows.shape[1]), jnp.float32)
    for member in members:
        width = member.shape[1]
        product_sum = product_sum + right_contract(shard_rows[:, cursor : cursor + width], member)
        cursor = cursor + width
    return (weight_acc, product_sum)


def body(tokens, norm_gain, attend_weight, up_weight, out_weight, down_weight, upstream):
    fin_size = lax.axis_size("fin")
    fin_index = lax.axis_index("fin")
    all_rows = tokens.shape[0]
    own_rows = all_rows // fin_size
    width_out = attend_weight.shape[2]
    local_heads = width_out // HEAD_DIM
    score_scale = HEAD_DIM ** (-0.5)
    inputs = tokens.astype(jnp.float32)
    row_sums, row_squares = lax.psum((jnp.sum(inputs, 1), jnp.sum(inputs * inputs, 1)), "fin")
    row_mean = row_sums[:, None] / D
    inv_scale = lax.rsqrt(row_squares[:, None] / D - row_mean * row_mean + EPS)
    centred = (inputs - row_mean) * inv_scale
    normed_rows = (centred * norm_gain[None, :]).astype(jnp.bfloat16)
    start_row = fin_index * own_rows
    query_image = (start_row + jnp.arange(own_rows, dtype=jnp.int32)) // SEQ
    key_image = jnp.arange(all_rows, dtype=jnp.int32) // SEQ
    image_mask = (query_image[:, None] == key_image[None, :]).astype(jnp.float32)
    full_members = (attend_weight[0], attend_weight[1], attend_weight[2], up_weight)
    projected = lax.psum_scatter(
        make_terms(normed_rows, full_members), "fin", scatter_dimension=0, tiled=True
    )
    query_raw = projected[:, :width_out]
    value_raw = projected[:, 2 * width_out : 3 * width_out]
    up_raw = projected[:, 3 * width_out :]
    key_normed, key_scales = head_norm(projected[:, width_out : 2 * width_out], local_heads)
    keys_all, values_all = (
        lax.all_gather(key_normed.astype(jnp.bfloat16), "fin", axis=0, tiled=True),
        lax.all_gather(value_raw.astype(jnp.bfloat16), "fin", axis=0, tiled=True),
    )
    query_normed, query_scales = head_norm(query_raw, local_heads)
    queries = query_normed.astype(jnp.bfloat16)
    query_split = queries.reshape(own_rows, local_heads, HEAD_DIM)
    key_split = keys_all.reshape(all_rows, local_heads, HEAD_DIM)
    value_split = values_all.reshape(all_rows, local_heads, HEAD_DIM)
    scores = (
        jnp.einsum("qhd,khd->hqk", query_split, key_split, preferred_element_type=jnp.float32)
        * score_scale
    )
    weights = jnp.exp(scores) * image_mask[None]
    probabilities = weights / jnp.sum(weights, -1, keepdims=True)
    probabilities_low = probabilities.astype(jnp.bfloat16)
    attended = (
        jnp.einsum(
            "hqk,khd->qhd", probabilities_low, value_split, preferred_element_type=jnp.float32
        )
        .reshape(own_rows, width_out)
        .astype(jnp.bfloat16)
    )
    activated = gelu_value(up_raw).astype(jnp.bfloat16)
    joined = jnp.concatenate([attended, activated], 1)
    shard_rows = lax.all_gather(joined, "fin", axis=0, tiled=True)
    branch_part = jnp.dot(
        shard_rows[:, :width_out], out_weight, preferred_element_type=jnp.float32
    ) + jnp.dot(shard_rows[:, width_out:], down_weight, preferred_element_type=jnp.float32)
    shard_rows = lax.all_gather(joined, "fin", axis=0, tiled=True)
    upstream_rows = upstream
    out_acc = left_contract(shard_rows[:, :width_out], upstream_rows)
    down_acc = left_contract(shard_rows[:, width_out:], upstream_rows)
    branch = lax.psum(branch_part.astype(jnp.bfloat16), "fout").astype(jnp.float32)
    layer_out = (inputs + branch).astype(jnp.bfloat16)
    upstream_rows = upstream
    joined_grad = lax.psum_scatter(
        jnp.concatenate(
            [right_contract(upstream_rows, out_weight), right_contract(upstream_rows, down_weight)],
            1,
        ),
        "fin",
        scatter_dimension=0,
        tiled=True,
    ).astype(jnp.bfloat16)
    attended_grad = joined_grad[:, :width_out].reshape(own_rows, local_heads, HEAD_DIM)
    up_grad_raw = joined_grad[:, width_out:].astype(jnp.float32) * gelu_slope(up_raw)
    prob_grad = jnp.einsum(
        "qhd,khd->hqk", attended_grad, value_split, preferred_element_type=jnp.float32
    )
    value_part = jnp.einsum(
        "hqk,qhd->khd", probabilities_low, attended_grad, preferred_element_type=jnp.float32
    ).reshape(all_rows, width_out)
    score_grad = (
        probabilities
        * (prob_grad - jnp.sum(prob_grad * probabilities, -1, keepdims=True))
        * score_scale
    ).astype(jnp.bfloat16)
    query_grad = jnp.einsum(
        "hqk,khd->qhd", score_grad, key_split, preferred_element_type=jnp.float32
    ).reshape(own_rows, width_out)
    key_part = jnp.einsum(
        "hqk,qhd->khd", score_grad, query_split, preferred_element_type=jnp.float32
    ).reshape(all_rows, width_out)
    query_grad = norm_back(query_grad, query_normed, query_scales, local_heads)
    key_own, value_own = (
        lax.psum_scatter(
            key_part.astype(jnp.bfloat16), "fin", scatter_dimension=0, tiled=True
        ).astype(jnp.float32),
        lax.psum_scatter(
            value_part.astype(jnp.bfloat16), "fin", scatter_dimension=0, tiled=True
        ).astype(jnp.float32),
    )
    key_grad = norm_back(key_own, key_normed, key_scales, local_heads)
    row_grads = jnp.concatenate([query_grad, key_grad, value_own, up_grad_raw], 1).astype(
        jnp.bfloat16
    )
    full_members = (attend_weight[0], attend_weight[1], attend_weight[2], up_weight)
    weight_acc, normed_grad = make_fold(
        normed_rows, full_members, lax.all_gather(row_grads, "fin", axis=0, tiled=True)
    )
    query_acc = weight_acc[:, :width_out]
    key_acc = weight_acc[:, width_out : 2 * width_out]
    value_acc = weight_acc[:, 2 * width_out : 3 * width_out]
    up_acc = weight_acc[:, 3 * width_out :]
    normed_grad = lax.psum(normed_grad.astype(jnp.bfloat16), "fout").astype(jnp.float32)
    gain_grad = jnp.sum(normed_grad * centred, 0)
    scaled_grad = normed_grad * norm_gain[None, :]
    grad_sum, grad_cross = lax.psum(
        (jnp.sum(scaled_grad, 1), jnp.sum(scaled_grad * centred, 1)), "fin"
    )
    inner = scaled_grad - grad_sum[:, None] / D - centred * (grad_cross[:, None] / D)
    tokens_grad = (upstream.astype(jnp.float32) + inv_scale * inner).astype(jnp.bfloat16)
    attend_grad = jnp.stack([query_acc, key_acc, value_acc]).astype(jnp.bfloat16)
    return (
        layer_out,
        tokens_grad,
        gain_grad,
        attend_grad,
        up_acc.astype(jnp.bfloat16),
        out_acc.astype(jnp.bfloat16),
        down_acc.astype(jnp.bfloat16),
    )


def solution(mesh):
    return jax.shard_map(
        body,
        mesh=mesh,
        in_specs=(
            P(None, "fin"),
            P("fin"),
            P(None, "fin", "fout"),
            P("fin", "fout"),
            P("fout", "fin"),
            P("fout", "fin"),
            P(None, "fin"),
        ),
        out_specs=(
            P(None, "fin"),
            P(None, "fin"),
            P("fin"),
            P(None, "fin", "fout"),
            P("fin", "fout"),
            P("fout", "fin"),
            P("fout", "fin"),
        ),
        check_vma=False,
    )
```

profile of v0, /device:TPU:1, one launch (start us, length us, event | category | flops | bytes accessed | tf_op | source)
XLA Modules:
  0.0 760.1 jit_solution(17420680256518740290)
XLA Ops:
  7.2 1.2 copy-done
  8.4 1.5 fusion.100
  10.3 1.4 pad_maximum_fusion.1
  11.8 0.8 copy-done.1
  12.8 39.7 %all-reduce.1 = (f32[256]{0:T(256)S(1)}, f32[256]{0:T(256)S(1)}) all-reduce(f32[256]{0:T(256)S(1)} %get-tuple-element.11, f32[256]{0:T(256)S(1)} %get-tuple-element.10), channel_id=1, replica_groups=mesh['fin'=16,'fout'=16] {'fin'}, use_global_device_ids=true, to_apply=%region_3.0 | all-reduce | flops 512 | bytes 4096 | tf_op jit(solution)/shard_map/psum | solution.py:84
  54.4 1.7 pad_maximum_fusion
  56.4 39.6 %reduce-scatter.7.cloned.1.call-done = f32[16,1920]{1,0:T(8,128)} async-done(((f32[256,1920]{1,0:T(8,128)}), f32[16,1920]{1,0:T(8,128)}) %reduce-scatter.7.cloned.1.call-update) | async-done | bytes 122896 | tf_op jit(solution)/shard_map/reduce_scatter | solution.py:137
  95.9 0.9 convert_element_type.110
  96.8 92.0 %reduce-scatter.5.cloned.1.call-done = f32[16,2688]{1,0:T(8,128)} async-done(((f32[256,2688]{1,0:T(8,128)}), f32[16,2688]{1,0:T(8,128)}) %reduce-scatter.5.cloned.1.call-update) | async-done | bytes 172048 | tf_op jit(solution)/shard_map/reduce_scatter | solution.py:94
  189.6 33.2 %all_gather.13 = bf16[256,384]{1,0:T(8,128)(2,1)S(1)} all-gather(bf16[16,384]{1,0:T(8,128)(2,1)S(1)} %slice.159), channel_id=1, replica_groups=mesh['fin'=16,'fout'=16] {'fin'}, dimensions={0}, use_global_device_ids=true | all-gather | bytes 208896 | tf_op jit(solution)/shard_map/all_gather | solution.py:103
  225.7 31.6 %all_gather.14 = bf16[256,384]{1,0:T(8,128)(2,1)S(1)} all-gather(bf16[16,384]{1,0:T(8,128)(2,1)S(1)} %get-tuple-element.30), channel_id=1, replica_groups=mesh['fin'=16,'fout'=16] {'fin'}, dimensions={0}, use_global_device_ids=true | all-gather | bytes 208896 | tf_op jit(solution)/shard_map/all_gather | solution.py:102
  258.2 0.8 copy.118
  259.3 0.8 copy.124
  260.7 94.4 %reduce-scatter.9.cloned.1.call-done = bf16[16,384]{1,0:T(8,128)(2,1)} async-done(((bf16[256,384]{1,0:T(8,128)(2,1)}), bf16[16,384]{1,0:T(8,128)(2,1)}) %reduce-scatter.9.cloned.1.call-update) | async-done | bytes 12304 | tf_op jit(solution)/shard_map/reduce_scatter | solution.py:167
  356.9 81.4 %reduce-scatter.11.cloned.1.call-done = bf16[16,384]{1,0:T(8,128)(2,1)} async-done(((bf16[256,384]{1,0:T(8,128)(2,1)}), bf16[16,384]{1,0:T(8,128)(2,1)}) %reduce-scatter.11.cloned.1.call-update) | async-done | bytes 12304 | tf_op jit(solution)/shard_map/reduce_scatter | solution.py:170
  438.3 1.3 pad_maximum_fusion.3
  439.9 43.0 %all_gather.15 = bf16[256,1920]{1,0:T(8,128)(2,1)S(1)} all-gather(bf16[16,1920]{1,0:T(8,128)(2,1)S(1)} %pad_maximum_fusion.4), channel_id=1, replica_groups=mesh['fin'=16,'fout'=16] {'fin'}, dimensions={0}, use_global_device_ids=true | all-gather | bytes 1044480 | tf_op jit(solution)/shard_map/all_gather | solution.py:126
  482.9 1.0 convolution_convert_fusion.2
  484.2 1.6 convolution_convert_fusion.1
  485.8 1.2 fusion.1
  487.0 37.2 %all-gather.2.cloned.1.call-done = bf16[256,2688]{1,0:T(8,128)(2,1)} async-done(((bf16[16,2688]{1,0:T(8,128)(2,1)}), bf16[256,2688]{1,0:T(8,128)(2,1)}) %all-gather.2.cloned.1.call-update) | async-done | bytes 1376272 | tf_op jit(solution)/shard_map/all_gather | solution.py:180
  524.2 1.5 fusion.34
  525.7 1.4 convolution_add_fusion.3
  527.2 1.2 convolution_add_fusion.2
  528.4 1.3 fusion.2
  529.7 0.9 convolution_convert_fusion
  530.6 1.1 slice.101
  531.8 1.0 pad_maximum_fusion.2
  532.8 183.1 %all-reduce.5.cloned.1.call-done = (bf16[256,384]{1,0:T(8,128)(2,1)}, bf16[256,384]{1,0:T(8,128)(2,1)}) async-done(((bf16[256,384]{1,0:T(8,128)(2,1)}, bf16[256,384]{1,0:T(8,128)(2,1)}), (bf16[256,384]{1,0:T(8,128)(2,1)}, bf16[256,384]{1,0:T(8,128)(2,1)})) %all-reduce.5.cloned.1.call-update) | async-done | bytes 393232 | tf_op jit(solution)/shard_map/psum | solution.py:134
  715.9 1.8 fusion.21
  717.7 33.5 %all-reduce = (f32[256]{0:T(256)S(1)}, f32[256]{0:T(256)S(1)}) all-reduce(f32[256]{0:T(256)S(1)} %get-tuple-element.8, f32[256]{0:T(256)S(1)} %get-tuple-element.9), channel_id=1, replica_groups=mesh['fin'=16,'fout'=16] {'fin'}, use_global_device_ids=true, to_apply=%region_23.24 | all-reduce | flops 512 | bytes 4096 | tf_op jit(solution)/shard_map/psum | solution.py:189
  751.3 2.0 fusion.19
  (83 shorter events, 10.2 us)
Async XLA Ops:
  7.2 1.3 copy-start
  7.2 2.8 copy-start.2
  7.2 2.8 copy-start.4
  7.2 88.7 %reduce-scatter.7.cloned.1.call-start = ((), (), s32[]{:S(2)}) async-start(), calls=%async_computation.5 | async-start | bytes 2088960 | tf_op jit(solution)/shard_map/reduce_scatter | solution.py:137
  11.7 0.9 copy-start.1
  11.7 40.8 %copy-start.7 = (bf16[3,384,384]{2,1,0:T(8,128)(2,1)S(1)}, bf16[3,384,384]{2,1,0:T(8,128)(2,1)}, u32[]{:S(2)}) copy-start(bf16[3,384,384]{2,1,0:T(8,128)(2,1)} %param.9) | copy-start | bytes 2654212
  11.7 40.8 %copy-start.9 = (f32[384]{0:T(512)S(1)}, f32[384]{0:T(512)}, u32[]{:S(2)}) copy-start(f32[384]{0:T(512)} %param.8) | copy-start | bytes 4612
  11.7 177.2 %reduce-scatter.5.cloned.1.call-start = ((), (), s32[]{:S(2)}) async-start(), calls=%async_computation.4 | async-start | bytes 2924544 | tf_op jit(solution)/shard_map/reduce_scatter | solution.py:94
  52.5 1.3 copy-start.5
  56.2 298.9 %reduce-scatter.9.cloned.1.call-start = ((), (), s32[]{:S(2)}) async-start(), calls=%async_computation.6 | async-start | bytes 208896 | tf_op jit(solution)/shard_map/reduce_scatter | solution.py:167
  257.5 3.2 copy-start.8
  259.0 179.3 %reduce-scatter.11.cloned.1.call-start = ((), (), s32[]{:S(2)}) async-start(), calls=%async_computation.7 | async-start | bytes 208896 | tf_op jit(solution)/shard_map/reduce_scatter | solution.py:170
  260.5 263.7 %all-gather.2.cloned.1.call-start = ((), (), s32[]{:S(2)}) async-start(), calls=%async_computation.8 | async-start | bytes 1462272 | tf_op jit(solution)/shard_map/all_gather | solution.py:180
  439.7 276.3 %all-reduce.5.cloned.1.call-start = ((), (), s32[]{:S(2)}) async-start(), calls=%async_computation.9 | async-start | bytes 786432 | tf_op jit(solution)/shard_map/psum | solution.py:134
  524.2 2.9 copy-start.3
  525.7 2.7 copy-start.6
Sparse Core Ops, SparseCore 0:
  11.8 84.0 reduce-scatter.6
  98.6 90.2 reduce-scatter.4
  259.1 95.9 reduce-scatter.8
  358.2 80.0 reduce-scatter.10
  440.5 83.6 all-gather.1
  529.8 186.0 all-reduce.4
where the time goes:
time: 768 us; the launch traced here: 760 us
  waiting for transfers between devices  528 us (69%)
  blocking collectives  181 us (24%)
  matrix products  15.2 us (2%)
  between operations  14.5 us (2%)
  other arithmetic  12.9 us (2%)
  local copies, waits for them, and re-layouts  8.42 us (1%)
    psum x1, waiting for transfers between devices, body(): lax.psum(branch_part.astype(jnp.bfloat16), 'fout').astype(jnp.float32)  183 us
    reduce_scatter x1, waiting for transfers between devices, body(): lax.psum_scatter(key_part.astype(jnp.bfloat16), 'fin', scatter_dimension=...  94.4 us
    reduce_scatter x1, waiting for transfers between devices, body(): lax.psum_scatter(make_terms(normed_rows, full_members), 'fin', scatter_di...  92 us
    reduce_scatter x1, waiting for transfers between devices, body(): lax.psum_scatter(value_part.astype(jnp.bfloat16), 'fin', scatter_dimensio...  81.4 us
    all_gather x1, blocking collectives, body(): shard_rows = lax.all_gather(joined, 'fin', axis=0, tiled=True)  43 us
    psum x1, blocking collectives, body(): lax.psum((jnp.sum(inputs, 1), jnp.sum(inputs * inputs, 1)), 'fin')  39.7 us
    reduce_scatter x1, waiting for transfers between devices, body(): lax.psum_scatter(jnp.concatenate([right_contract(upstream_rows, out_weigh...  39.6 us
    all_gather x1, waiting for transfers between devices, body(): lax.all_gather(row_grads, 'fin', axis=0, tiled=True)  37.2 us
  transfers between devices with their start and end apart: 6, of which 6 were waited for; matrix products, arithmetic and copies ran while one was open for 2% of the time, Pallas kernels for 0%

commit v1 on v0

v1 whole, which is shorter than its diff:
```python
import jax
import jax.numpy as jnp
from jax import lax
from jax.experimental import pallas as pl
from jax.experimental.pallas import tpu as pltpu
from jax.sharding import PartitionSpec as P

D = 6144
HEAD_DIM = 128
T = 256
W = 384
FF = 1536
EPS = 1e-06
BF = jnp.bfloat16
F32 = jnp.float32
MESH = pl.DeviceIdType.MESH
HIGH = lax.Precision.HIGHEST

ACT1 = 1024
ACT2 = FF - ACT1
UP1 = 768
UP2 = FF - UP1
CHUNKS = {"c0": W + ACT1, "c1": 3 * W, "c2": UP1, "c3": UP2, "c4": ACT2}
GROUPS = {"a0": 4 * W, "a1": UP1, "a2": UP2, "a3": ACT1, "a4": ACT2}


def scratch_shapes():
    shapes = {
        "tok": ((T, W), BF),
        "gain": ((1, W), F32),
        "aw": ((3, W, W), BF),
        "uw": ((W, FF), BF),
        "ow": ((W, W), BF),
        "dw": ((FF, W), BF),
        "ups": ((T, W), BF),
        "stz": ((4, 8, T), F32),
        "sty": ((4, 8, T), F32),
        "nr": ((T, W), BF),
        "nrt": ((W, T), BF),
        "cen": ((T, W), F32),
        "inv": ((T, 128), F32),
        "rawup": ((16, FF), F32),
        "actg": ((16, FF), F32),
        "attg": ((16, W), BF),
        "att": ((T, W), BF),
        "low": ((3, T, W), BF),
        "ng": ((T, W), F32),
        "og_v": ((W, W), BF),
        "dg_v": ((FF, W), BF),
        "ag_v": ((3, W, W), BF),
        "ug_v": ((W, FF), BF),
        "lo_v": ((T, W), BF),
        "tg_v": ((T, W), BF),
        "gg_v": ((1, W), F32),
        "fsy": ((4, 8, T), F32),
        "fsz": ((4, 8, T), F32),
        "fsc": ((2, 8, T), F32),
        "fsx": ((4, 8, T), F32),
        "fsh": ((2, 8, T), F32),
    }
    for name, w in CHUNKS.items():
        shapes[name + "P"] = ((T, w), BF)
        shapes[name + "R1"] = ((2, 32, w), BF)
        shapes[name + "R2"] = ((2, 64, w), BF)
        shapes[name + "T"] = ((2, 32, w), BF)
        shapes[name + "S"] = ((64, w), BF)
        shapes[name + "Z"] = ((3, 16, w), BF)
    for name, w in GROUPS.items():
        shapes[name + "G"] = ((T, w), BF)
    for name in ("b", "n"):
        shapes[name + "Q"] = ((T, W), BF)
        shapes[name + "AC"] = ((128, W), BF)
        shapes[name + "H1"] = ((128, W), BF)
        shapes[name + "AX"] = ((3, 32, W), BF)
        shapes[name + "H2"] = ((32, W), BF)
        shapes[name + "AZ"] = ((32, W), BF)
        shapes[name + "R"] = ((T, W), BF)
    return shapes


SHAPES = scratch_shapes()
N_COPIES = 140


def nt(a, b, **kw):
    return lax.dot_general(a, b, (((1,), (1,)), ((), ())), preferred_element_type=F32, **kw)


def tn(a, b):
    return lax.dot_general(a, b, (((0,), (0,)), ((), ())), preferred_element_type=F32)


def nn(a, b):
    return jnp.dot(a, b, preferred_element_type=F32)


def rows(start, size):
    return pl.ds(pl.multiple_of(start, 16), size)


def kernel(tok_h, gain_h, aw_h, uw_h, ow_h, dw_h, ups_h, lo_h, tg_h, gg_h, ag_out, ug_h, og_h, dg_h, *scr):
    s = dict(zip(SHAPES, scr[: len(SHAPES)]))
    send_sem, recv_sem, load_sem, store_sem = scr[len(SHAPES) :]

    f = lax.axis_index("fin")
    g = lax.axis_index("fout")
    y, z = f // 4, f % 4
    x, h, c = g // 4, (g // 2) % 2, g % 2

    def fin_dev(yy, zz):
        return (yy * 4 + zz, g)

    def fout_dev(xx, hh, cc):
        return (f, xx * 4 + hh * 2 + cc)

    right, left = lax.rem(y + 1, 4), lax.rem(y + 3, 4)
    far = lax.rem(y + 2, 4)
    dev_right, dev_left = fin_dev(right, z), fin_dev(left, z)
    y_devs = [fin_dev(lax.rem(y + d, 4), z) for d in (1, 2, 3)]
    z_devs = [fin_dev(y, lax.rem(z + d, 4)) for d in (1, 2, 3)]
    x_devs = [fout_dev(lax.rem(x + d, 4), h, c) for d in (1, 2, 3)]
    h_dev = fout_dev(x, 1 - h, c)
    c_dev = fout_dev(x, h, 1 - c)
    peers = y_devs + z_devs + x_devs + [h_dev, c_dev]

    loads = {}
    for i, (name, src) in enumerate(
        [("tok", tok_h), ("ups", ups_h), ("ow", ow_h), ("dw", dw_h), ("gain", gain_h), ("aw", aw_h), ("uw", uw_h)]
    ):
        loads[name] = pltpu.make_async_copy(src, s[name], load_sem.at[i])
        loads[name].start()

    barrier = pltpu.get_barrier_semaphore()
    for dev in peers:
        pl.semaphore_signal(barrier, inc=1, device_id=dev, device_id_type=MESH)

    copies = []
    stores = []

    def rcopy(src, dst, dev):
        i = len(copies)
        cp = pltpu.make_async_remote_copy(
            src_ref=src,
            dst_ref=dst,
            send_sem=send_sem.at[i],
            recv_sem=recv_sem.at[i],
            device_id=dev,
            device_id_type=MESH,
        )
        cp.start()
        copies.append(cp)
        return cp

    def store(src, dst):
        cp = pltpu.make_async_copy(src, dst, store_sem.at[len(stores)])
        cp.start()
        stores.append(cp)

    pending = {}

    def rs_a(n):
        p, r1, r2 = s[n + "P"], s[n + "R1"], s[n + "R2"]
        pending[n + "r1"] = [
            rcopy(p.at[rows(far * 64, 32)], r1.at[0], dev_right),
            rcopy(p.at[rows(far * 64 + 32, 32)], r1.at[1], dev_left),
        ]
        pending[n + "r2"] = [
            rcopy(p.at[rows(right * 64 + 32, 32)], r2.at[0, pl.ds(32, 32)], dev_right),
            rcopy(p.at[rows(left * 64, 32)], r2.at[1, pl.ds(0, 32)], dev_left),
        ]

    def rs_b(n):
        p, r1, r2, t = s[n + "P"], s[n + "R1"], s[n + "R2"], s[n + "T"]
        first, second = pending[n + "r1"]
        first.wait_recv()
        t[0] = (p[rows(right * 64, 32)].astype(F32) + r1[0].astype(F32)).astype(BF)
        pending[n + "r2"].append(rcopy(t.at[0], r2.at[0, pl.ds(0, 32)], dev_right))
        second.wait_recv()
        t[1] = (p[rows(left * 64 + 32, 32)].astype(F32) + r1[1].astype(F32)).astype(BF)
        pending[n + "r2"].append(rcopy(t.at[1], r2.at[1, pl.ds(32, 32)], dev_left))

    def rs_c(n):
        p, r2, sm, zz = s[n + "P"], s[n + "R2"], s[n + "S"], s[n + "Z"]
        for cp in pending[n + "r2"]:
            cp.wait_recv()
        sm[...] = (p[rows(y * 64, 64)].astype(F32) + r2[0].astype(F32) + r2[1].astype(F32)).astype(BF)
        pending[n + "z"] = [
            rcopy(sm.at[rows(lax.rem(z + d, 4) * 16, 16)], zz.at[d - 1], z_devs[d - 1]) for d in (1, 2, 3)
        ]

    def rs_d(n):
        sm, zz = s[n + "S"], s[n + "Z"]
        for cp in pending[n + "z"]:
            cp.wait_recv()
        return (
            sm[rows(z * 16, 16)].astype(F32) + zz[0].astype(F32) + zz[1].astype(F32) + zz[2].astype(F32)
        )

    def ag_e(n):
        gr = s[n + "G"]
        own = gr.at[rows(f * 16, 16)]
        pending[n + "e"] = [rcopy(own, own, dev) for dev in z_devs]

    def ag_f(n):
        gr = s[n + "G"]
        for cp in pending[n + "e"]:
            cp.wait_recv()
        block = gr.at[rows(y * 64, 64)]
        pending[n + "f"] = [rcopy(block, block, dev_right), rcopy(block, block, dev_left)]

    def ag_h(n):
        gr = s[n + "G"]
        first, second = pending[n + "f"]
        first.wait_recv()
        one = gr.at[rows(left * 64, 32)]
        cps = [rcopy(one, one, dev_right)]
        second.wait_recv()
        two = gr.at[rows(right * 64 + 32, 32)]
        cps.append(rcopy(two, two, dev_left))
        pending[n + "h"] = cps

    def ag_i(n):
        for cp in pending[n + "h"]:
            cp.wait_recv()

    def ar_1(n):
        q = s[n + "Q"]
        pending[n + "1"] = rcopy(q.at[rows((1 - c) * 128, 128)], s[n + "AC"], c_dev)

    def ar_2(n):
        q, h1, ax = s[n + "Q"], s[n + "H1"], s[n + "AX"]
        pending[n + "1"].wait_recv()
        h1[...] = (q[rows(c * 128, 128)].astype(F32) + s[n + "AC"][...].astype(F32)).astype(BF)
        pending[n + "2"] = [
            rcopy(h1.at[rows(lax.rem(x + d, 4) * 32, 32)], ax.at[d - 1], x_devs[d - 1]) for d in (1, 2, 3)
        ]

    def ar_3(n):
        h1, ax, h2 = s[n + "H1"], s[n + "AX"], s[n + "H2"]
        for cp in pending[n + "2"]:
            cp.wait_recv()
        h2[...] = (
            h1[rows(x * 32, 32)].astype(F32) + ax[0].astype(F32) + ax[1].astype(F32) + ax[2].astype(F32)
        ).astype(BF)
        pending[n + "3"] = rcopy(h2, s[n + "AZ"], h_dev)

    def ar_4(n):
        res = s[n + "R"]
        pending[n + "3"].wait_recv()
        at = rows(c * 128 + x * 32, 32)
        res[at] = (s[n + "H2"][...].astype(F32) + s[n + "AZ"][...].astype(F32)).astype(BF)
        pending[n + "4"] = [rcopy(res.at[at], res.at[at], dev) for dev in x_devs]

    def ar_5(n):
        res = s[n + "R"]
        for cp in pending[n + "4"]:
            cp.wait_recv()
        at = res.at[rows(c * 128, 128)]
        pending[n + "5"] = rcopy(at, at, c_dev)

    def ar_6(n):
        pending[n + "5"].wait_recv()
        return s[n + "R"][...].astype(F32)

    def ex_start(buf, value, slot, devs):
        buf[slot] = value
        return [rcopy(buf.at[slot], buf.at[slot], dev) for dev in devs]

    def ex_sum(buf, cps):
        for cp in cps:
            cp.wait_recv()
        return sum(buf[i] for i in range(1, buf.shape[0])) + buf[0]

    row_id = lax.broadcasted_iota(jnp.int32, (8, W), 0)
    pick0 = jnp.where(row_id == 0, 1.0, 0.0).astype(F32)
    pick1 = jnp.where(row_id == 1, 1.0, 0.0).astype(F32)

    def pair_sums(first, second):
        return nt(pick0, first, precision=HIGH) + nt(pick1, second, precision=HIGH)

    loads["tok"].wait()
    inputs = s["tok"][...].astype(F32)
    stats = pair_sums(inputs, inputs * inputs)
    loads["ups"].wait()
    loads["ow"].wait()
    loads["dw"].wait()
    pl.semaphore_wait(barrier, len(peers))
    st_cps = ex_start(s["stz"], stats, z, z_devs)

    ups = s["ups"][...]
    s["c0P"][:, 0:W] = nt(ups, s["ow"][...]).astype(BF)
    for i in range(0, ACT1, 512):
        s["c0P"][:, W + i : W + i + 512] = nt(ups, s["dw"][i : i + 512, :]).astype(BF)
    rs_a("c0")
    stats = ex_sum(s["stz"], st_cps)
    st_cps = ex_start(s["sty"], stats, y, y_devs)
    s["c4P"][...] = nt(ups, s["dw"][ACT1:FF, :]).astype(BF)
    rs_b("c0")
    stats = ex_sum(s["sty"], st_cps)
    columns = jnp.concatenate([stats] * 16, 0).T
    row_mean = columns[:, 0:1] / D
    inv_scale = lax.rsqrt(columns[:, 1:2] / D - row_mean * row_mean + EPS)
    centred = (inputs - row_mean) * inv_scale
    s["cen"][...] = centred
    s["inv"][...] = jnp.broadcast_to(inv_scale, (T, 128))
    loads["gain"].wait()
    normed = (centred * s["gain"][...]).astype(BF)
    s["nr"][...] = normed
    loads["aw"].wait()
    for i in range(3):
        s["c1P"][:, i * W : (i + 1) * W] = nn(normed, s["aw"][i]).astype(BF)
    rs_a("c1")
    loads["uw"].wait()
    for i in range(0, UP1, 384):
        s["c2P"][:, i : i + 384] = nn(normed, s["uw"][:, i : i + 384]).astype(BF)
    rs_a("c2")
    rs_c("c0")
    rs_b("c1")
    for i in range(0, UP2, 384):
        s["c3P"][:, i : i + 384] = nn(normed, s["uw"][:, UP1 + i : UP1 + i + 384]).astype(BF)
    rs_a("c3")
    rs_a("c4")
    rs_b("c2")
    rs_c("c1")
    part = rs_d("c0")
    s["attg"][...] = part[:, 0:W].astype(BF)
    s["actg"][:, 0:ACT1] = part[:, W:].astype(BF).astype(F32)
    rs_b("c3")
    rs_c("c2")
    own = rows(f * 16, 16)
    s["a0G"][own, 0 : 3 * W] = rs_d("c1").astype(BF)
    s["a0G"][own, 3 * W : 4 * W] = s["attg"][...]
    ag_e("a0")
    rs_b("c4")
    rs_c("c3")

    def gelu_value(v):
        return 0.5 * v * (1.0 + lax.erf(v * 0.7071067811865476))

    def gelu_slope(v):
        return (
            0.5 * (1.0 + lax.erf(v * 0.7071067811865476)) + v * jnp.exp(-0.5 * v * v) * 0.3989422804014327
        )

    part = rs_d("c2")
    s["rawup"][:, 0:UP1] = part
    s["a1G"][own, :] = gelu_value(part).astype(BF)
    ag_e("a1")
    ag_f("a0")
    rs_c("c4")
    part = rs_d("c3")
    s["rawup"][:, UP1:FF] = part
    s["a2G"][own, :] = gelu_value(part).astype(BF)
    ag_e("a2")
    s["a3G"][own, :] = (s["actg"][:, 0:ACT1] * gelu_slope(s["rawup"][:, 0:ACT1])).astype(BF)
    ag_e("a3")
    ag_f("a1")
    part = rs_d("c4").astype(BF).astype(F32)
    s["a4G"][own, :] = (part * gelu_slope(s["rawup"][:, ACT1:FF])).astype(BF)
    ag_e("a4")
    ag_h("a0")
    ag_f("a2")
    ag_h("a1")
    ag_f("a3")
    ag_i("a0")

    score_scale = HEAD_DIM ** (-0.5)

    def head_norm(v):
        cent = v - jnp.mean(v, -1, keepdims=True)
        scale = lax.rsqrt(jnp.mean(cent * cent, -1, keepdims=True) + EPS)
        return cent * scale, scale

    def norm_back(gr, normed_v, scale):
        return scale * (
            gr - jnp.mean(gr, -1, keepdims=True) - normed_v * jnp.mean(gr * normed_v, -1, keepdims=True)
        )

    def head(i):
        lo = i * HEAD_DIM
        hi = lo + HEAD_DIM
        gr = s["a0G"]
        qn, qs = head_norm(gr[:, lo:hi].astype(F32))
        kn, ks = head_norm(gr[:, W + lo : W + hi].astype(F32))
        v = gr[:, 2 * W + lo : 2 * W + hi]
        da = gr[:, 3 * W + lo : 3 * W + hi]
        q, k = qn.astype(BF), kn.astype(BF)
        e = jnp.exp(nt(q, k) * score_scale)
        p = e / jnp.sum(e, -1, keepdims=True)
        pl_ = p.astype(BF)
        s["att"][:, lo:hi] = nn(pl_, v).astype(BF)
        dp = nt(da, v)
        ds = (p * (dp - jnp.sum(dp * p, -1, keepdims=True)) * score_scale).astype(BF)
        s["low"][0, :, lo:hi] = norm_back(nn(ds, k), qn, qs).astype(BF)
        s["low"][1, :, lo:hi] = norm_back(tn(ds, q), kn, ks).astype(BF)
        s["low"][2, :, lo:hi] = tn(pl_, da).astype(BF)

    head(0)
    ag_h("a2")
    ag_f("a4")
    head(1)
    ag_h("a3")
    head(2)
    ag_i("a1")
    ag_i("a2")
    branch = nn(s["att"][...], s["ow"][...])
    branch += nn(s["a1G"][...], s["dw"][0:UP1, :])
    branch += nn(s["a2G"][...], s["dw"][UP1:FF, :])
    s["bQ"][...] = branch.astype(BF)
    ar_1("b")
    ag_h("a4")
    ngrad = nt(s["low"][0], s["aw"][0]) + nt(s["low"][1], s["aw"][1]) + nt(s["low"][2], s["aw"][2])
    s["ng"][...] = ngrad
    ar_2("b")
    s["nrt"][...] = s["nr"][...].T
    for i in range(3):
        s["ag_v"][i] = nn(s["nrt"][...], s["low"][i]).astype(BF)
    store(s["ag_v"], ag_out)
    ar_3("b")
    ag_i("a3")
    ngrad = s["ng"][...] + nt(s["a3G"][...], s["uw"][:, 0:ACT1])
    ag_i("a4")
    ngrad = ngrad + nt(s["a4G"][...], s["uw"][:, ACT1:FF])
    s["nQ"][...] = ngrad.astype(BF)
    ar_1("n")
    scaled = ngrad * s["gain"][...]
    sums = pair_sums(scaled, scaled * s["cen"][...])
    sm_cps = ex_start(s["fsy"], sums, y, y_devs)
    ar_2("n")
    s["og_v"][...] = tn(s["att"][...], ups).astype(BF)
    store(s["og_v"], og_h)
    for i in range(0, ACT1, 512):
        s["ug_v"][:, i : i + 512] = nn(s["nrt"][...], s["a3G"][:, i : i + 512]).astype(BF)
    ar_4("b")
    sums = ex_sum(s["fsy"], sm_cps)
    sm_cps = ex_start(s["fsz"], sums, z, z_devs)
    ar_3("n")
    s["ug_v"][:, ACT1:FF] = nn(s["nrt"][...], s["a4G"][...]).astype(BF)
    store(s["ug_v"], ug_h)
    sums = ex_sum(s["fsz"], sm_cps)
    sm_cps = ex_start(s["fsc"], sums, c, [c_dev])
    for i in range(0, UP1, 384):
        s["dg_v"][i : i + 384, :] = tn(s["a1G"][:, i : i + 384], ups).astype(BF)
    sums = ex_sum(s["fsc"], sm_cps)
    sm_cps = ex_start(s["fsx"], sums, x, x_devs)
    ar_4("n")
    ar_5("b")
    for i in range(0, UP2, 384):
        s["dg_v"][UP1 + i : UP1 + i + 384, :] = tn(s["a2G"][:, i : i + 384], ups).astype(BF)
    store(s["dg_v"], dg_h)
    sums = ex_sum(s["fsx"], sm_cps)
    sm_cps = ex_start(s["fsh"], sums, h, [h_dev])
    ar_5("n")
    s["lo_v"][...] = (s["tok"][...].astype(F32) + ar_6("b")).astype(BF)
    store(s["lo_v"], lo_h)
    sums = ex_sum(s["fsh"], sm_cps)
    columns = jnp.concatenate([sums] * 16, 0).T
    grad_mean = columns[:, 0:1] / D
    grad_cross = columns[:, 1:2] / D
    ngrad = ar_6("n")
    centred = s["cen"][...]
    s["gg_v"][...] = jnp.sum(ngrad * centred, 0, keepdims=True)
    store(s["gg_v"], gg_h)
    inner = ngrad * s["gain"][...] - grad_mean - centred * grad_cross
    s["tg_v"][...] = (ups.astype(F32) + s["inv"][:, 0:1] * inner).astype(BF)
    store(s["tg_v"], tg_h)

    for cp in copies:
        cp.wait_send()
    for cp in stores:
        cp.wait()


def body(tokens, norm_gain, attend_weight, up_weight, out_weight, down_weight, upstream):
    any_spec = pl.BlockSpec(memory_space=pl.ANY)
    outs = pl.pallas_call(
        kernel,
        out_shape=(
            jax.ShapeDtypeStruct((T, W), BF),
            jax.ShapeDtypeStruct((T, W), BF),
            jax.ShapeDtypeStruct((1, W), F32),
            jax.ShapeDtypeStruct((3, W, W), BF),
            jax.ShapeDtypeStruct((W, FF), BF),
            jax.ShapeDtypeStruct((W, W), BF),
            jax.ShapeDtypeStruct((FF, W), BF),
        ),
        in_specs=[any_spec] * 7,
        out_specs=(any_spec,) * 7,
        scratch_shapes=[pltpu.VMEM(shape, dtype) for shape, dtype in SHAPES.values()]
        + [
            pltpu.SemaphoreType.DMA((N_COPIES,)),
            pltpu.SemaphoreType.DMA((N_COPIES,)),
            pltpu.SemaphoreType.DMA((8,)),
            pltpu.SemaphoreType.DMA((8,)),
        ],
        compiler_params=pltpu.CompilerParams(
            collective_id=0, has_side_effects=True, vmem_limit_bytes=56 * 1024 * 1024
        ),
        name="layer",
    )(tokens, norm_gain.reshape(1, W), attend_weight, up_weight, out_weight, down_weight, upstream)
    layer_out, tokens_grad, gain_grad, attend_grad, up_grad, out_grad, down_grad = outs
    return (layer_out, tokens_grad, gain_grad.reshape(W), attend_grad, up_grad, out_grad, down_grad)


def solution(mesh):
    return jax.shard_map(
        body,
        mesh=mesh,
        in_specs=(
            P(None, "fin"),
            P("fin"),
            P(None, "fin", "fout"),
            P("fin", "fout"),
            P("fout", "fin"),
            P("fout", "fin"),
            P(None, "fin"),
        ),
        out_specs=(
            P(None, "fin"),
            P(None, "fin"),
            P("fin"),
            P(None, "fin", "fout"),
            P("fin", "fout"),
            P("fout", "fin"),
            P("fout", "fin"),
        ),
        check_vma=False,
    )
```

time: 768 us -> 100 us (0.13); the launches traced: 760 us -> 99.9 us
  waiting for transfers between devices: 528 us -> 0 us
  blocking collectives: 181 us -> 0 us
  Pallas kernels: 0 us -> 88.4 us
  matrix products: 15.2 us -> 0 us
  between operations: 14.5 us -> 0.65 us
  other arithmetic: 12.9 us -> 1.28 us
    reduce_scatter x4 -> x0, waiting for transfers between devices: 307 us -> none  [the longest x1 94.4 us: body(): lax.psum_scatter(key_part.astype(jnp.bfloat16), 'fin', scatter_dimension=...]
    psum x1 -> x0, waiting for transfers between devices: 183 us -> none  [body(): lax.psum(branch_part.astype(jnp.bfloat16), 'fout').astype(jnp.float32)]
    all_gather x3 -> x0, blocking collectives: 108 us -> none  [the longest x1 43 us: body(): shard_rows = lax.all_gather(joined, 'fin', axis=0, tiled=True)]
    pallas_call x0 -> x1, Pallas kernels: none -> 88.4 us  [body(): pl.pallas_call(kernel, out_shape=(jax.ShapeDtypeStruct((T, W), BF), jax.S...]
    psum x2 -> x0, blocking collectives: 73.3 us -> none  [the longest x1 39.7 us: body(): lax.psum((jnp.sum(inputs, 1), jnp.sum(inputs * inputs, 1)), 'fin')]
    all_gather x1 -> x0, waiting for transfers between devices: 37.2 us -> none  [body(): lax.all_gather(row_grads, 'fin', axis=0, tiled=True)]
    dot_general x20 -> x0, matrix products: 15 us -> none  [the longest x6 7.22 us: right_contract(): lax.dot_general(left, right, (((1,), (1,)), ((), ())), preferred_element_...]
  transfers between devices with their start and end apart: 6 -> 0, of which waited for: 6 -> 0; matrix products, arithmetic and copies ran while one was open for 2% -> 0% of each run, Pallas kernels for 0% -> 0%
where the time goes in v1:
time: 100 us; the launch traced here: 99.9 us
  Pallas kernels  88.4 us (88%)
  local copies, waits for them, and re-layouts  9.61 us (10%)
  other arithmetic  1.28 us (1%)
    pallas_call x1, Pallas kernels, body(): pl.pallas_call(kernel, out_shape=(jax.ShapeDtypeStruct((T, W), BF), jax.S...  88.4 us
    unnamed x12, local copies, waits for them, and re-layouts  8.37 us

profile of v1, /device:TPU:1, one launch (start us, length us, event | category | flops | bytes accessed | tf_op | source)
XLA Modules:
  0.0 99.9 jit_solution(14951620355632078584)
XLA Ops:
  0.6 1.2 %reshape.20.gain_h = f32[1,384]{1,0:T(1,128)} reshape(f32[384]{0:T(512)} %param.8) | data formatting | bytes 3072 | tf_op jit(solution)/shard_map/reshape | solution.py:500
  1.9 88.4 %layer.1 = (bf16[256,384]{1,0:T(8,128)(2,1)}, bf16[256,384]{1,0:T(8,128)(2,1)}, f32[1,384]{1,0:T(1,128)}, bf16[3,384,384]{2,1,0:T(8,128)(2,1)}, bf16[384,1536]{1...) custom-call(bf16[256,384]{1,0:T(8,128)(2,1)} %tok_h.1, f32[1,384]{1,0:T(1,128)} %reshape.20.gain_h, ...), custom_call_target="tpu_custom_call" | custom-call | tf_op jit(solution)/shard_map/layer/pallas_call | solution.py:476
  90.3 1.3 %reduce = f32[384]{0:T(512)} reduce(f32[1,384]{1,0:T(1,128)} %get-tuple-element.16, f32[]{:T(128)} %constant), dimensions={0}, to_apply=%get-tuple-element.16.reduce_sub_computation | reduce | bytes 3076 | tf_op jit(solution)/shard_map/layer/pallas_call | solution.py:476
  91.5 1.6 %copy.20 = bf16[256,384]{1,0:T(8,128)(2,1)} copy(bf16[256,384]{1,0:T(8,128)(2,1)} %get-tuple-element.28) | data formatting | bytes 393216
  93.2 0.0 copy-start.1
  93.2 1.7 %copy.21 = bf16[256,384]{1,0:T(8,128)(2,1)} copy(bf16[256,384]{1,0:T(8,128)(2,1)} %get-tuple-element.29) | data formatting | bytes 393216
  94.9 2.2 %copy.22 = bf16[3,384,384]{2,1,0:T(8,128)(2,1)} copy(bf16[3,384,384]{2,1,0:T(8,128)(2,1)} %get-tuple-element.31) | data formatting | bytes 1769472
  97.1 0.0 copy-done.1
  97.1 0.0 copy-start.2
  97.1 0.0 copy-start
  97.1 1.0 %copy.23 = bf16[384,1536]{1,0:T(8,128)(2,1)} copy(bf16[384,1536]{1,0:T(8,128)(2,1)S(1)} %copy-done.1) | data formatting | bytes 2359296
  98.1 0.1 copy-done.2
  98.2 0.7 copy.24
  98.9 0.0 copy-done
  98.9 1.0 %copy.25 = bf16[1536,384]{1,0:T(8,128)(2,1)} copy(bf16[1536,384]{1,0:T(8,128)(2,1)S(1)} %copy-done) | data formatting | bytes 2359296
Async XLA Ops:
  93.2 3.9 %copy-start.1 = (bf16[384,1536]{1,0:T(8,128)(2,1)S(1)}, bf16[384,1536]{1,0:T(8,128)(2,1)}, u32[]{:S(2)}) copy-start(bf16[384,1536]{1,0:T(8,128)(2,1)} %get-tuple-element.32) | copy-start | bytes 3538948
  97.1 1.1 %copy-start.2 = (bf16[384,384]{1,0:T(8,128)(2,1)S(1)}, bf16[384,384]{1,0:T(8,128)(2,1)}, u32[]{:S(2)}) copy-start(bf16[384,384]{1,0:T(8,128)(2,1)} %get-tuple-element.33) | copy-start | bytes 884740
  97.1 1.8 %copy-start = (bf16[1536,384]{1,0:T(8,128)(2,1)S(1)}, bf16[1536,384]{1,0:T(8,128)(2,1)}, u32[]{:S(2)}) copy-start(bf16[1536,384]{1,0:T(8,128)(2,1)} %get-tuple-element.34) | copy-start | bytes 3538948

commit v2 on v1

--- a/solution.py
+++ b/solution.py
@@ -27,7 +27,7 @@
 def scratch_shapes():
     shapes = {
         "tok": ((T, W), BF),
-        "gain": ((1, W), F32),
+        "gain": ((W,), F32),
         "aw": ((3, W, W), BF),
         "uw": ((W, FF), BF),
         "ow": ((W, W), BF),
@@ -45,13 +45,6 @@
         "att": ((T, W), BF),
         "low": ((3, T, W), BF),
         "ng": ((T, W), F32),
-        "og_v": ((W, W), BF),
-        "dg_v": ((FF, W), BF),
-        "ag_v": ((3, W, W), BF),
-        "ug_v": ((W, FF), BF),
-        "lo_v": ((T, W), BF),
-        "tg_v": ((T, W), BF),
-        "gg_v": ((1, W), F32),
         "fsy": ((4, 8, T), F32),
         "fsz": ((4, 8, T), F32),
         "fsc": ((2, 8, T), F32),
@@ -98,9 +91,11 @@
     return pl.ds(pl.multiple_of(start, 16), size)
 
 
-def kernel(tok_h, gain_h, aw_h, uw_h, ow_h, dw_h, ups_h, lo_h, tg_h, gg_h, ag_out, ug_h, og_h, dg_h, *scr):
+def kernel(tok_h, gain_h, aw_h, uw_h, ow_h, dw_h, ups_h, *refs):
+    outs, scr = refs[:7], refs[7:]
     s = dict(zip(SHAPES, scr[: len(SHAPES)]))
-    send_sem, recv_sem, load_sem, store_sem = scr[len(SHAPES) :]
+    s.update(zip(("lo_v", "tg_v", "gg_v", "ag_v", "ug_v", "og_v", "dg_v"), outs))
+    send_sem, recv_sem, load_sem = scr[len(SHAPES) :]
 
     f = lax.axis_index("fin")
     g = lax.axis_index("fout")
@@ -135,7 +130,6 @@
         pl.semaphore_signal(barrier, inc=1, device_id=dev, device_id_type=MESH)
 
     copies = []
-    stores = []
 
     def rcopy(src, dst, dev):
         i = len(copies)
@@ -151,11 +145,6 @@
         copies.append(cp)
         return cp
 
-    def store(src, dst):
-        cp = pltpu.make_async_copy(src, dst, store_sem.at[len(stores)])
-        cp.start()
-        stores.append(cp)
-
     pending = {}
 
     def rs_a(n):
@@ -281,20 +270,20 @@
     loads["tok"].wait()
     inputs = s["tok"][...].astype(F32)
     stats = pair_sums(inputs, inputs * inputs)
+
     loads["ups"].wait()
     loads["ow"].wait()
     loads["dw"].wait()
-    pl.semaphore_wait(barrier, len(peers))
-    st_cps = ex_start(s["stz"], stats, z, z_devs)
-
     ups = s["ups"][...]
     s["c0P"][:, 0:W] = nt(ups, s["ow"][...]).astype(BF)
     for i in range(0, ACT1, 512):
         s["c0P"][:, W + i : W + i + 512] = nt(ups, s["dw"][i : i + 512, :]).astype(BF)
+    s["c4P"][...] = nt(ups, s["dw"][ACT1:FF, :]).astype(BF)
+    pl.semaphore_wait(barrier, len(peers))
+    st_cps = ex_start(s["stz"], stats, z, z_devs)
     rs_a("c0")
     stats = ex_sum(s["stz"], st_cps)
     st_cps = ex_start(s["sty"], stats, y, y_devs)
-    s["c4P"][...] = nt(ups, s["dw"][ACT1:FF, :]).astype(BF)
     rs_b("c0")
     stats = ex_sum(s["sty"], st_cps)
     columns = jnp.concatenate([stats] * 16, 0).T
@@ -304,7 +293,7 @@
     s["cen"][...] = centred
     s["inv"][...] = jnp.broadcast_to(inv_scale, (T, 128))
     loads["gain"].wait()
-    normed = (centred * s["gain"][...]).astype(BF)
+    normed = (centred * s["gain"][...][None, :]).astype(BF)
     s["nr"][...] = normed
     loads["aw"].wait()
     for i in range(3):
@@ -415,7 +404,6 @@
     s["nrt"][...] = s["nr"][...].T
     for i in range(3):
         s["ag_v"][i] = nn(s["nrt"][...], s["low"][i]).astype(BF)
-    store(s["ag_v"], ag_out)
     ar_3("b")
     ag_i("a3")
     ngrad = s["ng"][...] + nt(s["a3G"][...], s["uw"][:, 0:ACT1])
@@ -423,12 +411,11 @@
     ngrad = ngrad + nt(s["a4G"][...], s["uw"][:, ACT1:FF])
     s["nQ"][...] = ngrad.astype(BF)
     ar_1("n")
-    scaled = ngrad * s["gain"][...]
+    scaled = ngrad * s["gain"][...][None, :]
     sums = pair_sums(scaled, scaled * s["cen"][...])
     sm_cps = ex_start(s["fsy"], sums, y, y_devs)
     ar_2("n")
     s["og_v"][...] = tn(s["att"][...], ups).astype(BF)
-    store(s["og_v"], og_h)
     for i in range(0, ACT1, 512):
         s["ug_v"][:, i : i + 512] = nn(s["nrt"][...], s["a3G"][:, i : i + 512]).astype(BF)
     ar_4("b")
@@ -436,7 +423,6 @@
     sm_cps = ex_start(s["fsz"], sums, z, z_devs)
     ar_3("n")
     s["ug_v"][:, ACT1:FF] = nn(s["nrt"][...], s["a4G"][...]).astype(BF)
-    store(s["ug_v"], ug_h)
     sums = ex_sum(s["fsz"], sm_cps)
     sm_cps = ex_start(s["fsc"], sums, c, [c_dev])
     for i in range(0, UP1, 384):
@@ -447,27 +433,30 @@
     ar_5("b")
     for i in range(0, UP2, 384):
         s["dg_v"][UP1 + i : UP1 + i + 384, :] = tn(s["a2G"][:, i : i + 384], ups).astype(BF)
-    store(s["dg_v"], dg_h)
     sums = ex_sum(s["fsx"], sm_cps)
     sm_cps = ex_start(s["fsh"], sums, h, [h_dev])
     ar_5("n")
     s["lo_v"][...] = (s["tok"][...].astype(F32) + ar_6("b")).astype(BF)
-    store(s["lo_v"], lo_h)
     sums = ex_sum(s["fsh"], sm_cps)
     columns = jnp.concatenate([sums] * 16, 0).T
     grad_mean = columns[:, 0:1] / D
     grad_cross = columns[:, 1:2] / D
     ngrad = ar_6("n")
     centred = s["cen"][...]
-    s["gg_v"][...] = jnp.sum(ngrad * centred, 0, keepdims=True)
-    store(s["gg_v"], gg_h)
-    inner = ngrad * s["gain"][...] - grad_mean - centred * grad_cross
+    s["gg_v"][...] = jnp.sum(ngrad * centred, 0)
+    inner = ngrad * s["gain"][...][None, :] - grad_mean - centred * grad_cross
     s["tg_v"][...] = (ups.astype(F32) + s["inv"][:, 0:1] * inner).astype(BF)
-    store(s["tg_v"], tg_h)
 
     for cp in copies:
         cp.wait_send()
-    for cp in stores:
+
+
+def hand_on(*refs):
+    sem = refs[-1]
+    cps = [pltpu.make_async_copy(refs[i], refs[7 + i], sem.at[i]) for i in range(7)]
+    for cp in cps:
+        cp.start()
+    for cp in cps:
         cp.wait()
 
 
@@ -476,30 +465,36 @@
     outs = pl.pallas_call(
         kernel,
         out_shape=(
-            jax.ShapeDtypeStruct((T, W), BF),
-            jax.ShapeDtypeStruct((T, W), BF),
-            jax.ShapeDtypeStruct((1, W), F32),
-            jax.ShapeDtypeStruct((3, W, W), BF),
-            jax.ShapeDtypeStruct((W, FF), BF),
-            jax.ShapeDtypeStruct((W, W), BF),
-            jax.ShapeDtypeStruct((FF, W), BF),
+            pltpu.VMEM((T, W), BF),
+            pltpu.VMEM((T, W), BF),
+            pltpu.VMEM((W,), F32),
+            pltpu.VMEM((3, W, W), BF),
+            pltpu.VMEM((W, FF), BF),
+            pltpu.VMEM((W, W), BF),
+            pltpu.VMEM((FF, W), BF),
         ),
         in_specs=[any_spec] * 7,
-        out_specs=(any_spec,) * 7,
+        out_specs=(pl.BlockSpec(memory_space=pltpu.VMEM),) * 7,
         scratch_shapes=[pltpu.VMEM(shape, dtype) for shape, dtype in SHAPES.values()]
         + [
             pltpu.SemaphoreType.DMA((N_COPIES,)),
             pltpu.SemaphoreType.DMA((N_COPIES,)),
             pltpu.SemaphoreType.DMA((8,)),
-            pltpu.SemaphoreType.DMA((8,)),
         ],
         compiler_params=pltpu.CompilerParams(
-            collective_id=0, has_side_effects=True, vmem_limit_bytes=56 * 1024 * 1024
+            collective_id=0, has_side_effects=True, vmem_limit_bytes=57 * 1024 * 1024
         ),
         name="layer",
-    )(tokens, norm_gain.reshape(1, W), attend_weight, up_weight, out_weight, down_weight, upstream)
-    layer_out, tokens_grad, gain_grad, attend_grad, up_grad, out_grad, down_grad = outs
-    return (layer_out, tokens_grad, gain_grad.reshape(W), attend_grad, up_grad, out_grad, down_grad)
+    )(tokens, norm_gain, attend_weight, up_weight, out_weight, down_weight, upstream)
+    return pl.pallas_call(
+        hand_on,
+        out_shape=tuple(jax.ShapeDtypeStruct(o.shape, o.dtype) for o in outs),
+        in_specs=[any_spec] * 7,
+        out_specs=(any_spec,) * 7,
+        scratch_shapes=[pltpu.SemaphoreType.DMA((7,))],
+        compiler_params=pltpu.CompilerParams(vmem_limit_bytes=2 * 1024 * 1024),
+        name="hand_on",
+    )(*outs)
 
 
 def solution(mesh):

time: 100 us -> 90.4 us (0.904)
  local copies, waits for them, and re-layouts: 9.61 us -> 0 us
  Pallas kernels: 88.4 us -> 89.7 us
  other arithmetic: 1.28 us -> 0 us
    unnamed x12 -> x0, local copies, waits for them, and re-layouts: 8.37 us -> none
    pallas_call x1 -> x2, Pallas kernels: 88.4 us -> 89.7 us  [the longest x1 87.7 us: body(): pl.pallas_call(kernel, out_shape=(pltpu.VMEM((T, W), BF), pltpu.VMEM((T,...]
    pallas_call x1 -> x0, other arithmetic: 1.28 us -> none  [body(): pl.pallas_call(kernel, out_shape=(jax.ShapeDtypeStruct((T, W), BF), jax.S...]
    reshape x1 -> x0, local copies, waits for them, and re-layouts: 1.25 us -> none  [body(): norm_gain.reshape(1, W)]
where the time goes in v2:
time: 90.4 us; the launch traced here: 90.3 us
  Pallas kernels  89.7 us (99%)
    pallas_call x1, Pallas kernels, body(): pl.pallas_call(kernel, out_shape=(pltpu.VMEM((T, W), BF), pltpu.VMEM((T,...  87.7 us
    pallas_call x1, Pallas kernels, body(): pl.pallas_call(hand_on, out_shape=tuple((jax.ShapeDtypeStruct(o.shape, o....  1.99 us

profile of v2, /device:TPU:1, one launch (start us, length us, event | category | flops | bytes accessed | tf_op | source)
XLA Modules:
  0.0 90.3 jit_solution(18299336600611882782)
XLA Ops:
  0.6 87.7 %layer.1 = (bf16[256,384]{1,0:T(8,128)(2,1)S(1)}, bf16[256,384]{1,0:T(8,128)(2,1)S(1)}, f32[384]{0:T(512)S(1)}, bf16[3,384,384]{2,1,0:T(8,128)(2,1)S(1)}, bf16[3...) custom-call(bf16[256,384]{1,0:T(8,128)(2,1)} %tok_h.1, f32[384]{0:T(512)} %gain_h.1, ...), custom_call_target="tpu_custom_call" | custom-call | tf_op jit(solution)/shard_map/layer/pallas_call | solution.py:465
  88.3 2.0 %hand_on.1 = (bf16[256,384]{1,0:T(8,128)(2,1)}, bf16[256,384]{1,0:T(8,128)(2,1)}, f32[384]{0:T(512)}, bf16[3,384,384]{2,1,0:T(8,128)(2,1)}, bf16[384,1536]{1,0:T...) custom-call(bf16[256,384]{1,0:T(8,128)(2,1)S(1)} %get-tuple-element.14.refs_0_, ...), custom_call_target="tpu_custom_call" | custom-call | tf_op jit(solution)/shard_map/hand_on/pallas_call | solution.py:489

commit v3 on v2

v3 whole, which is shorter than its diff:
```python
import jax
import jax.numpy as jnp
from jax import lax
from jax.experimental import pallas as pl
from jax.experimental.pallas import tpu as pltpu
from jax.sharding import PartitionSpec as P

D = 6144
HEAD_DIM = 128
T = 256
W = 384
FF = 1536
EPS = 1e-06
BF = jnp.bfloat16
F32 = jnp.float32
MESH = pl.DeviceIdType.MESH
HIGH = lax.Precision.HIGHEST

WIDE = 1024
NARROW = FF - WIDE
UP = ((0, WIDE), (WIDE, NARROW))
HEADS = (0, 1, 2)
CHUNKS = {"h1": 512, "h2": 512, "u0": WIDE, "u1": NARROW, "d0": WIDE, "d1": NARROW}
GROUPS = {"h0": 512, "h1": 512, "h2": 512, "a0": WIDE, "a1": NARROW, "l0": WIDE}


def scratch_shapes():
    shapes = {
        "tok": ((T, W), BF),
        "gain": ((W,), F32),
        "aw": ((3, W, W), BF),
        "uw": ((W, FF), BF),
        "ow": ((W, W), BF),
        "dw": ((FF, W), BF),
        "ups": ((T, W), BF),
        "st": ((16, 8, 128), F32),
        "wg": ((4, 24, 128), F32),
        "wz": ((4, 8, 128), F32),
        "h0P": ((4, 4, 16, 512), BF),
        "h0Z": ((3, 4, 16, 512), BF),
        "h0S": ((4, 16, 512), BF),
        "h0Y": ((3, 16, 512), BF),
        "l1G": ((4, 4, 16, NARROW), BF),
        "col": ((T, 128), F32),
        "nrt": ((W, T), BF),
        "cen": ((T, W), F32),
        "rawup": ((16, FF), F32),
        "att": ((T, W), BF),
        "low": ((3, T, W), BF),
        "ng": ((T, W), F32),
        "fa": ((16, 8, 128), F32),
        "fb": ((2, 8, 128), F32),
        "fc": ((8, 8, 128), F32),
    }
    for name, w in CHUNKS.items():
        shapes[name + "P"] = ((T, w), BF)
        shapes[name + "R1"] = ((2, 32, w), BF)
        shapes[name + "R2"] = ((2, 64, w), BF)
        shapes[name + "T"] = ((2, 32, w), BF)
        shapes[name + "S"] = ((64, w), BF)
        shapes[name + "Z"] = ((3, 16, w), BF)
    for name, w in GROUPS.items():
        shapes[name + "G"] = ((T, w), BF)
    for name in ("b", "n"):
        shapes[name + "Q"] = ((T, W), BF)
        shapes[name + "AC"] = ((128, W), BF)
        shapes[name + "H1"] = ((128, W), BF)
        shapes[name + "AX"] = ((7, 16, W), BF)
        shapes[name + "R"] = ((T, W), BF)
    return shapes


SHAPES = scratch_shapes()
N_COPIES = 200


def nt(a, b, **kw):
    return lax.dot_general(a, b, (((1,), (1,)), ((), ())), preferred_element_type=F32, **kw)


def tn(a, b):
    return lax.dot_general(a, b, (((0,), (0,)), ((), ())), preferred_element_type=F32)


def nn(a, b):
    return jnp.dot(a, b, preferred_element_type=F32)


def rows(start, size):
    return pl.ds(pl.multiple_of(start, 16), size)


def kernel(tok_h, gain_h, aw_h, uw_h, ow_h, dw_h, ups_h, *refs):
    outs, scr = refs[:7], refs[7:]
    s = dict(zip(SHAPES, scr[: len(SHAPES)]))
    s.update(zip(("lo_v", "tg_v", "gg_v", "ag_v", "ug_v", "og_v", "dg_v"), outs))
    send_sem, recv_sem, load_sem = scr[len(SHAPES) :]

    f = lax.axis_index("fin")
    g = lax.axis_index("fout")
    y, z = f // 4, f % 4
    x, h, c = g // 4, (g // 2) % 2, g % 2

    def fin_dev(yy, zz):
        return (yy * 4 + zz, g)

    def fout_dev(xx, hh, cc):
        return (f, xx * 4 + hh * 2 + cc)

    right, left = lax.rem(y + 1, 4), lax.rem(y + 3, 4)
    far = lax.rem(y + 2, 4)
    dev_right, dev_left = fin_dev(right, z), fin_dev(left, z)
    y_devs = [fin_dev(lax.rem(y + d, 4), z) for d in (1, 2, 3)]
    z_devs = [fin_dev(y, lax.rem(z + d, 4)) for d in (1, 2, 3)]
    xh = x * 2 + h
    xh_devs = []
    for d in range(1, 8):
        other = lax.rem(xh + d, 8)
        xh_devs.append(fout_dev(other // 2, lax.rem(other, 2), c))
    c_dev = fout_dev(x, h, 1 - c)
    fin_devs = [(lax.rem(f + d, 16), g) for d in range(1, 16)]
    peers = fin_devs + xh_devs + [c_dev]

    loads = {}
    for i, (name, src) in enumerate(
        [("tok", tok_h), ("gain", gain_h), ("aw", aw_h), ("ups", ups_h), ("ow", ow_h), ("uw", uw_h), ("dw", dw_h)]
    ):
        loads[name] = pltpu.make_async_copy(src, s[name], load_sem.at[i])
        loads[name].start()

    barrier = pltpu.get_barrier_semaphore()
    for dev in peers:
        pl.semaphore_signal(barrier, inc=1, device_id=dev, device_id_type=MESH)

    copies = []

    def rcopy(src, dst, dev):
        i = len(copies)
        cp = pltpu.make_async_remote_copy(
            src_ref=src,
            dst_ref=dst,
            send_sem=send_sem.at[i],
            recv_sem=recv_sem.at[i],
            device_id=dev,
            device_id_type=MESH,
        )
        cp.start()
        copies.append(cp)
        return cp

    pending = {}

    def rs_a(n):
        p, r1, r2 = s[n + "P"], s[n + "R1"], s[n + "R2"]
        pending[n + "r1"] = [
            rcopy(p.at[rows(far * 64, 32)], r1.at[0], dev_right),
            rcopy(p.at[rows(far * 64 + 32, 32)], r1.at[1], dev_left),
        ]
        pending[n + "r2"] = [
            rcopy(p.at[rows(right * 64 + 32, 32)], r2.at[0, pl.ds(32, 32)], dev_right),
            rcopy(p.at[rows(left * 64, 32)], r2.at[1, pl.ds(0, 32)], dev_left),
        ]

    def rs_b(n):
        p, r1, r2, t = s[n + "P"], s[n + "R1"], s[n + "R2"], s[n + "T"]
        first, second = pending[n + "r1"]
        first.wait_recv()
        t[0] = (p[rows(right * 64, 32)].astype(F32) + r1[0].astype(F32)).astype(BF)
        pending[n + "r2"].append(rcopy(t.at[0], r2.at[0, pl.ds(0, 32)], dev_right))
        second.wait_recv()
        t[1] = (p[rows(left * 64 + 32, 32)].astype(F32) + r1[1].astype(F32)).astype(BF)
        pending[n + "r2"].append(rcopy(t.at[1], r2.at[1, pl.ds(32, 32)], dev_left))

    def rs_c(n, blocks=()):
        p, r2, sm, zz = s[n + "P"], s[n + "R2"], s[n + "S"], s[n + "Z"]
        for cp in pending[n + "r2"]:
            cp.wait_recv()
        total = p[rows(y * 64, 64)].astype(F32) + r2[0].astype(F32) + r2[1].astype(F32)
        if blocks:
            shift = s["col"][rows(y * 64, 64), :]
            shift = [jnp.broadcast_to(shift[:, 2 + i : 3 + i], (64, 128)) for i in range(4)]
            parts = [
                sum(shift[i] * s["wg"][i, b : b + 1, :] for i in range(4)) for b in blocks
            ]
            wide = len(blocks) * 128
            sm[:, 0:wide] = (total[:, 0:wide] + jnp.concatenate(parts, 1)).astype(BF)
            if wide < total.shape[1]:
                sm[:, wide:] = total[:, wide:].astype(BF)
        else:
            sm[...] = total.astype(BF)
        pending[n + "z"] = [
            rcopy(sm.at[rows(lax.rem(z + d, 4) * 16, 16)], zz.at[d - 1], z_devs[d - 1]) for d in (1, 2, 3)
        ]

    def rs_d(n):
        sm, zz = s[n + "S"], s[n + "Z"]
        for cp in pending[n + "z"]:
            cp.wait_recv()
        return (
            sm[rows(z * 16, 16)].astype(F32) + zz[0].astype(F32) + zz[1].astype(F32) + zz[2].astype(F32)
        )

    def rs_za(n):
        p = s[n + "P"]
        pending[n + "z"] = [
            rcopy(p.at[:, lax.rem(z + d, 4)], s[n + "Z"].at[d - 1], z_devs[d - 1]) for d in (1, 2, 3)
        ]

    def rs_zc(n, blocks):
        p, zz, sm = s[n + "P"], s[n + "Z"], s[n + "S"]
        for cp in pending[n + "z"]:
            cp.wait_recv()
        for q in range(4):
            total = p[q, z].astype(F32) + zz[0, q].astype(F32) + zz[1, q].astype(F32) + zz[2, q].astype(F32)
            shift = s["col"][rows(q * 64 + z * 16, 16), :]
            shift = [jnp.broadcast_to(shift[:, 6 + i : 7 + i], (16, 128)) for i in range(4)]
            parts = [sum(shift[i] * s["wz"][i, b : b + 1, :] for i in range(4)) for b in blocks]
            wide = len(blocks) * 128
            sm[q, :, 0:wide] = (total[:, 0:wide] + jnp.concatenate(parts, 1)).astype(BF)
            sm[q, :, wide:] = total[:, wide:].astype(BF)
        pending[n + "y"] = [
            rcopy(sm.at[lax.rem(y + d, 4)], s[n + "Y"].at[d - 1], y_devs[d - 1]) for d in (1, 2, 3)
        ]

    def rs_zd(n):
        yy = s[n + "Y"]
        for cp in pending[n + "y"]:
            cp.wait_recv()
        return s[n + "S"][y].astype(F32) + yy[0].astype(F32) + yy[1].astype(F32) + yy[2].astype(F32)

    def ag_ye(n):
        own_block = s[n + "G"].at[y, z]
        pending[n + "e"] = [rcopy(own_block, own_block, dev) for dev in y_devs]

    def ag_yf(n):
        for cp in pending[n + "e"]:
            cp.wait_recv()
        block = s[n + "G"].at[:, z]
        pending[n + "h"] = [rcopy(block, block, dev) for dev in z_devs]

    def ag_e(n):
        gr = s[n + "G"]
        own = gr.at[rows(f * 16, 16)]
        pending[n + "e"] = [rcopy(own, own, dev) for dev in z_devs]

    def ag_f(n):
        gr = s[n + "G"]
        for cp in pending[n + "e"]:
            cp.wait_recv()
        block = gr.at[rows(y * 64, 64)]
        pending[n + "f"] = [rcopy(block, block, dev_right), rcopy(block, block, dev_left)]

    def ag_h(n):
        gr = s[n + "G"]
        first, second = pending[n + "f"]
        first.wait_recv()
        one = gr.at[rows(left * 64, 32)]
        cps = [rcopy(one, one, dev_right)]
        second.wait_recv()
        two = gr.at[rows(right * 64 + 32, 32)]
        cps.append(rcopy(two, two, dev_left))
        pending[n + "h"] = cps

    def ag_i(n):
        for cp in pending[n + "h"]:
            cp.wait_recv()

    def ar_1(n):
        q = s[n + "Q"]
        pending[n + "1"] = rcopy(q.at[rows((1 - c) * 128, 128)], s[n + "AC"], c_dev)

    def ar_2(n):
        q, h1, ax = s[n + "Q"], s[n + "H1"], s[n + "AX"]
        pending[n + "1"].wait_recv()
        h1[...] = (q[rows(c * 128, 128)].astype(F32) + s[n + "AC"][...].astype(F32)).astype(BF)
        pending[n + "2"] = [
            rcopy(h1.at[rows(lax.rem(xh + d, 8) * 16, 16)], ax.at[d - 1], xh_devs[d - 1]) for d in range(1, 8)
        ]

    def ar_3(n):
        h1, ax, res = s[n + "H1"], s[n + "AX"], s[n + "R"]
        for cp in pending[n + "2"]:
            cp.wait_recv()
        total = h1[rows(xh * 16, 16)].astype(F32) + sum(ax[i].astype(F32) for i in range(7))
        at = rows(c * 128 + xh * 16, 16)
        res[at] = total.astype(BF)
        pending[n + "3"] = [rcopy(res.at[at], res.at[at], dev) for dev in xh_devs]

    def ar_4(n):
        res = s[n + "R"]
        for cp in pending[n + "3"]:
            cp.wait_recv()
        at = res.at[rows(c * 128, 128)]
        pending[n + "4"] = rcopy(at, at, c_dev)

    def ar_5(n):
        pending[n + "4"].wait_recv()
        return s[n + "R"][...].astype(F32)

    def ex_start(buf, value, slot, devs):
        one = buf.at[slot]
        one[0:2, :] = value[0:2, 0:128]
        one[2:4, :] = value[0:2, 128:256]
        return [rcopy(one, one, dev) for dev in devs]

    def ex_sum(buf, cps):
        for cp in cps:
            cp.wait_recv()
        total = sum(buf[i] for i in range(buf.shape[0]))
        return jnp.concatenate([total[0:2, :], total[2:4, :]], 1)

    row_id = lax.broadcasted_iota(jnp.int32, (8, W), 0)
    pick0 = jnp.where(row_id == 0, 1.0, 0.0).astype(F32)
    pick1 = jnp.where(row_id == 1, 1.0, 0.0).astype(F32)

    def pair_sums(first, second):
        return nt(pick0, first, precision=HIGH) + nt(pick1, second, precision=HIGH)

    loads["tok"].wait()
    inputs = s["tok"][...].astype(F32)
    stats = pair_sums(inputs, inputs * inputs)
    stat = s["st"].at[f]
    stat[0:2, :] = stats[0:2, 0:128]
    stat[2:4, :] = stats[0:2, 128:256]
    local = (inputs - jnp.mean(inputs, 1, keepdims=True))
    loads["gain"].wait()
    gain = s["gain"][...][None, :]
    local = (local * gain).astype(BF)
    gain_high = gain.astype(BF).astype(F32)
    row16 = lax.broadcasted_iota(jnp.int32, (16, W), 0)
    gain_rows = jnp.where(row16 == 0, gain_high, jnp.where(row16 == 1, gain - gain_high, 0.0)).astype(BF)
    wg = s["wg"].at[y]
    wz = s["wz"].at[z]

    def gain_product(weight):
        both = nn(gain_rows, weight)
        return both[0:1, :] + both[1:2, :]

    loads["aw"].wait()
    for i in range(3):
        line = gain_product(s["aw"][i])
        part = nn(local, s["aw"][i]).astype(BF)
        for k in HEADS:
            wg[3 * k + i : 3 * k + i + 1, :] = line[:, k * 128 : (k + 1) * 128]
        wz[i : i + 1, :] = line[:, 0:128]
        s["h0P"][:, :, :, i * 128 : (i + 1) * 128] = part[:, 0:128].reshape(4, 4, 16, 128)
        for k in (1, 2):
            s[f"h{k}P"][:, i * 128 : (i + 1) * 128] = part[:, k * 128 : (k + 1) * 128]
    loads["ups"].wait()
    loads["ow"].wait()
    ups = s["ups"][...]
    part = nt(ups, s["ow"][...]).astype(BF)
    s["h0P"][:, :, :, W:512] = part[:, 0:128].reshape(4, 4, 16, 128)
    for k in (1, 2):
        s[f"h{k}P"][:, W:512] = part[:, k * 128 : (k + 1) * 128]
    loads["uw"].wait()
    for i in range(4):
        line = gain_product(s["uw"][:, i * W : (i + 1) * W])
        for k in range(3):
            wg[9 + 3 * i + k : 10 + 3 * i + k, :] = line[:, k * 128 : (k + 1) * 128]

    def up_product(k):
        for i in range(0, UP[k][1], 512):
            at = UP[k][0] + i
            s[f"u{k}P"][:, i : i + 512] = nn(local, s["uw"][:, at : at + 512]).astype(BF)

    def down_product(k):
        for i in range(0, UP[k][1], 512):
            at = UP[k][0] + i
            s[f"d{k}P"][:, i : i + 512] = nt(ups, s["dw"][at : at + 512, :]).astype(BF)

    up_product(0)
    pl.semaphore_wait(barrier, len(peers))
    rs_za("h0")
    st_cps = [rcopy(stat, stat, dev) for dev in fin_devs]
    wg_cps = [rcopy(wg, wg, dev) for dev in y_devs]
    rs_a("h1")
    rs_a("h2")
    wg_cps += [rcopy(wz, wz, dev) for dev in z_devs]
    rs_a("u0")
    up_product(1)
    rs_b("h1")
    rs_a("u1")
    for cp in st_cps:
        cp.wait_recv()
    total = sum(s["st"][i] for i in range(16))
    mean_row = jnp.concatenate([total[0:1, :], total[2:3, :]], 1) / D
    square_row = jnp.concatenate([total[1:2, :], total[3:4, :]], 1) / D
    inv_row = lax.rsqrt(square_row - mean_row * mean_row + EPS)
    lines = [mean_row, inv_row]
    for i in range(8):
        one = s["st"][i * 4 + z] if i < 4 else s["st"][y * 4 + i - 4]
        lines.append(jnp.concatenate([one[0:1, :], one[2:3, :]], 1) / W - mean_row)
    lines += [mean_row] * 6
    s["col"][...] = jnp.concatenate(lines * 8, 0).T
    rs_b("h2")
    loads["dw"].wait()
    down_product(0)
    rs_a("d0")
    for cp in wg_cps:
        cp.wait_recv()
    rs_zc("h0", (0, 1, 2))
    rs_b("u0")
    rs_c("h1", (3, 4, 5))
    down_product(1)
    rs_a("d1")
    rs_b("u1")
    rs_c("h2", (6, 7, 8))
    own = rows(f * 16, 16)
    own_inv = s["col"][own, 1:2]

    def head_rows(k):
        part = rs_d(f"h{k}") if k else rs_zd("h0")
        s[f"h{k}G"][own, 0:W] = (part[:, 0:W] * own_inv).astype(BF)
        s[f"h{k}G"][own, W:512] = part[:, W:512].astype(BF)
        ag_e(f"h{k}")

    def up_rows(k):
        part = rs_d(f"u{k}") * own_inv
        s["rawup"][:, UP[k][0] : UP[k][0] + UP[k][1]] = part
        s[f"a{k}G"][own, :] = gelu_value(part).astype(BF)
        ag_e(f"a{k}")

    def low_rows(k):
        part = rs_d(f"d{k}").astype(BF).astype(F32)
        part = (part * gelu_slope(s["rawup"][:, UP[k][0] : UP[k][0] + UP[k][1]])).astype(BF)
        if k == 0:
            s["l0G"][own, :] = part
            ag_e("l0")
        else:
            s["l1G"][y, z] = part
            ag_ye("l1")

    def gelu_value(v):
        return 0.5 * v * (1.0 + lax.erf(v * 0.7071067811865476))

    def gelu_slope(v):
        return (
            0.5 * (1.0 + lax.erf(v * 0.7071067811865476)) + v * jnp.exp(-0.5 * v * v) * 0.3989422804014327
        )

    head_rows(0)
    rs_b("d0")
    head_rows(1)
    rs_c("u0", tuple(range(9, 17)))
    rs_b("d1")
    head_rows(2)
    rs_c("u1", tuple(range(17, 21)))
    ag_f("h0")
    rs_c("d0")
    ag_f("h1")
    rs_c("d1")
    up_rows(0)
    ag_f("h2")
    up_rows(1)
    ag_h("h0")
    low_rows(0)
    ag_h("h1")
    low_rows(1)
    ag_f("a0")
    ag_h("h2")
    ag_f("a1")
    ag_i("h0")
    centred = (inputs - s["col"][:, 0:1]) * s["col"][:, 1:2]
    s["cen"][...] = centred
    normed = (centred * gain).astype(BF)
    s["nrt"][...] = normed.T
    ag_f("l0")
    ag_yf("l1")
    ag_h("a0")

    score_scale = HEAD_DIM ** (-0.5)

    def head_norm(v):
        cent = v - jnp.mean(v, -1, keepdims=True)
        scale = lax.rsqrt(jnp.mean(cent * cent, -1, keepdims=True) + EPS)
        return cent * scale, scale

    def norm_back(gr, normed_v, scale):
        return scale * (
            gr - jnp.mean(gr, -1, keepdims=True) - normed_v * jnp.mean(gr * normed_v, -1, keepdims=True)
        )

    def head(i):
        lo = i * HEAD_DIM
        hi = lo + HEAD_DIM
        gr = s[f"h{i}G"]
        qn, qs = head_norm(gr[:, 0:128].astype(F32))
        kn, ks = head_norm(gr[:, 128:256].astype(F32))
        v = gr[:, 256:384]
        da = gr[:, 384:512]
        q, k = qn.astype(BF), kn.astype(BF)
        e = jnp.exp(nt(q, k) * score_scale)
        p = e / jnp.sum(e, -1, keepdims=True)
        pl_ = p.astype(BF)
        s["att"][:, lo:hi] = nn(pl_, v).astype(BF)
        dp = nt(da, v)
        ds = (p * (dp - jnp.sum(dp * p, -1, keepdims=True)) * score_scale).astype(BF)
        s["low"][0, :, lo:hi] = norm_back(nn(ds, k), qn, qs).astype(BF)
        s["low"][1, :, lo:hi] = norm_back(tn(ds, q), kn, ks).astype(BF)
        s["low"][2, :, lo:hi] = tn(pl_, da).astype(BF)

    head(0)
    ag_h("a1")
    ag_i("h1")
    head(1)
    ag_h("l0")
    ag_i("h2")
    head(2)
    ag_i("a0")
    branch = nn(s["att"][...], s["ow"][...]) + nn(s["a0G"][...], s["dw"][0:WIDE, :])
    ag_i("a1")
    s["bQ"][...] = (branch + nn(s["a1G"][...], s["dw"][WIDE:FF, :])).astype(BF)
    ar_1("b")
    ngrad = nt(s["low"][0], s["aw"][0]) + nt(s["low"][1], s["aw"][1]) + nt(s["low"][2], s["aw"][2])
    ag_i("l0")
    s["ng"][...] = ngrad + nt(s["l0G"][...], s["uw"][:, 0:WIDE])
    ar_2("b")
    ag_i("l1")
    l1_rows = s["l1G"][...].reshape(T, NARROW)
    ngrad = s["ng"][...] + nt(l1_rows, s["uw"][:, WIDE:FF])
    s["nQ"][...] = ngrad.astype(BF)
    ar_1("n")
    scaled = ngrad * gain
    sums = pair_sums(scaled, scaled * s["cen"][...])
    sm_cps = ex_start(s["fa"], sums, f, fin_devs)
    ar_2("n")
    for i in range(3):
        s["ag_v"][i] = nn(s["nrt"][...], s["low"][i]).astype(BF)
    s["og_v"][...] = tn(s["att"][...], ups).astype(BF)
    ar_3("b")
    sums = ex_sum(s["fa"], sm_cps)
    sm_cps = ex_start(s["fb"], sums, c, [c_dev])
    ar_3("n")
    sums = ex_sum(s["fb"], sm_cps)
    sm_cps = ex_start(s["fc"], sums, xh, xh_devs)
    for i in (0, 512):
        s["ug_v"][:, i : i + 512] = nn(s["nrt"][...], s["l0G"][:, i : i + 512]).astype(BF)
    s["ug_v"][:, WIDE:FF] = nn(s["nrt"][...], l1_rows).astype(BF)
    ar_4("b")
    for i in (0, 512):
        s["dg_v"][i : i + 512, :] = tn(s["a0G"][:, i : i + 512], ups).astype(BF)
    s["dg_v"][WIDE:FF, :] = tn(s["a1G"][...], ups).astype(BF)
    s["lo_v"][...] = (s["tok"][...].astype(F32) + ar_5("b")).astype(BF)
    ar_4("n")
    sums = ex_sum(s["fc"], sm_cps)
    columns = jnp.concatenate([sums] * 64, 0).T
    grad_mean = columns[:, 0:1] / D
    grad_cross = columns[:, 1:2] / D
    ngrad = ar_5("n")
    centred = s["cen"][...]
    s["gg_v"][...] = jnp.sum(ngrad * centred, 0)
    inner = ngrad * gain - grad_mean - centred * grad_cross
    s["tg_v"][...] = (ups.astype(F32) + s["col"][:, 1:2] * inner).astype(BF)

    for cp in copies:
        cp.wait_send()


def hand_on(*refs):
    sem = refs[-1]
    cps = [pltpu.make_async_copy(refs[i], refs[7 + i], sem.at[i]) for i in range(7)]
    for cp in cps:
        cp.start()
    for cp in cps:
        cp.wait()


def body(tokens, norm_gain, attend_weight, up_weight, out_weight, down_weight, upstream):
    any_spec = pl.BlockSpec(memory_space=pl.ANY)
    outs = pl.pallas_call(
        kernel,
        out_shape=(
            pltpu.VMEM((T, W), BF),
            pltpu.VMEM((T, W), BF),
            pltpu.VMEM((W,), F32),
            pltpu.VMEM((3, W, W), BF),
            pltpu.VMEM((W, FF), BF),
            pltpu.VMEM((W, W), BF),
            pltpu.VMEM((FF, W), BF),
        ),
        in_specs=[any_spec] * 7,
        out_specs=(pl.BlockSpec(memory_space=pltpu.VMEM),) * 7,
        scratch_shapes=[pltpu.VMEM(shape, dtype) for shape, dtype in SHAPES.values()]
        + [
            pltpu.SemaphoreType.DMA((N_COPIES,)),
            pltpu.SemaphoreType.DMA((N_COPIES,)),
            pltpu.SemaphoreType.DMA((8,)),
        ],
        compiler_params=pltpu.CompilerParams(
            collective_id=0, has_side_effects=True, vmem_limit_bytes=57 * 1024 * 1024
        ),
        name="layer",
    )(tokens, norm_gain, attend_weight, up_weight, out_weight, down_weight, upstream)
    return pl.pallas_call(
        hand_on,
        out_shape=tuple(jax.ShapeDtypeStruct(o.shape, o.dtype) for o in outs),
        in_specs=[any_spec] * 7,
        out_specs=(any_spec,) * 7,
        scratch_shapes=[pltpu.SemaphoreType.DMA((7,))],
        compiler_params=pltpu.CompilerParams(vmem_limit_bytes=2 * 1024 * 1024),
        name="hand_on",
    )(*outs)


def solution(mesh):
    return jax.shard_map(
        body,
        mesh=mesh,
        in_specs=(
            P(None, "fin"),
            P("fin"),
            P(None, "fin", "fout"),
            P("fin", "fout"),
            P("fout", "fin"),
            P("fout", "fin"),
            P(None, "fin"),
        ),
        out_specs=(
            P(None, "fin"),
            P(None, "fin"),
            P("fin"),
            P(None, "fin", "fout"),
            P("fin", "fout"),
            P("fout", "fin"),
            P("fout", "fin"),
        ),
        check_vma=False,
    )
```

time: 90.4 us -> 83.6 us (0.925)
  Pallas kernels: 89.7 us -> 82.9 us
    pallas_call x1, Pallas kernels: 87.7 us -> 80.9 us  [body(): pl.pallas_call(kernel, out_shape=(pltpu.VMEM((T, W), BF), pltpu.VMEM((T,...]
where the time goes in v3:
time: 83.6 us; the launch traced here: 83.5 us
  Pallas kernels  82.9 us (99%)
    pallas_call x1, Pallas kernels, body(): pl.pallas_call(kernel, out_shape=(pltpu.VMEM((T, W), BF), pltpu.VMEM((T,...  80.9 us
    pallas_call x1, Pallas kernels, body(): pl.pallas_call(hand_on, out_shape=tuple((jax.ShapeDtypeStruct(o.shape, o....  1.99 us

profile of v3, /device:TPU:1, one launch (start us, length us, event | category | flops | bytes accessed | tf_op | source)
XLA Modules:
  0.0 83.5 jit_solution(11363516752210369792)
XLA Ops:
  0.6 80.9 %layer.1 = (bf16[256,384]{1,0:T(8,128)(2,1)S(1)}, bf16[256,384]{1,0:T(8,128)(2,1)S(1)}, f32[384]{0:T(512)S(1)}, bf16[3,384,384]{2,1,0:T(8,128)(2,1)S(1)}, bf16[3...) custom-call(bf16[256,384]{1,0:T(8,128)(2,1)} %tok_h.1, f32[384]{0:T(512)} %gain_h.1, ...), custom_call_target="tpu_custom_call" | custom-call | tf_op jit(solution)/shard_map/layer/pallas_call | solution.py:571
  81.5 2.0 %hand_on.1 = (bf16[256,384]{1,0:T(8,128)(2,1)}, bf16[256,384]{1,0:T(8,128)(2,1)}, f32[384]{0:T(512)}, bf16[3,384,384]{2,1,0:T(8,128)(2,1)}, bf16[384,1536]{1,0:T...) custom-call(bf16[256,384]{1,0:T(8,128)(2,1)S(1)} %get-tuple-element.14.refs_0_, ...), custom_call_target="tpu_custom_call" | custom-call | tf_op jit(solution)/shard_map/hand_on/pallas_call | solution.py:595

commit v4 on v3

--- a/solution.py
+++ b/solution.py
@@ -16,7 +16,7 @@
 MESH = pl.DeviceIdType.MESH
 HIGH = lax.Precision.HIGHEST
 
-WIDE = 1024
+WIDE = 768
 NARROW = FF - WIDE
 UP = ((0, WIDE), (WIDE, NARROW))
 HEADS = (0, 1, 2)
@@ -360,63 +360,29 @@
             wg[9 + 3 * i + k : 10 + 3 * i + k, :] = line[:, k * 128 : (k + 1) * 128]
 
     def up_product(k):
-        for i in range(0, UP[k][1], 512):
+        for i in range(0, UP[k][1], W):
             at = UP[k][0] + i
-            s[f"u{k}P"][:, i : i + 512] = nn(local, s["uw"][:, at : at + 512]).astype(BF)
+            s[f"u{k}P"][:, i : i + W] = nn(local, s["uw"][:, at : at + W]).astype(BF)
 
     def down_product(k):
-        for i in range(0, UP[k][1], 512):
+        for i in range(0, UP[k][1], W):
             at = UP[k][0] + i
-            s[f"d{k}P"][:, i : i + 512] = nt(ups, s["dw"][at : at + 512, :]).astype(BF)
-
-    up_product(0)
-    pl.semaphore_wait(barrier, len(peers))
-    rs_za("h0")
-    st_cps = [rcopy(stat, stat, dev) for dev in fin_devs]
-    wg_cps = [rcopy(wg, wg, dev) for dev in y_devs]
-    rs_a("h1")
-    rs_a("h2")
-    wg_cps += [rcopy(wz, wz, dev) for dev in z_devs]
-    rs_a("u0")
-    up_product(1)
-    rs_b("h1")
-    rs_a("u1")
-    for cp in st_cps:
-        cp.wait_recv()
-    total = sum(s["st"][i] for i in range(16))
-    mean_row = jnp.concatenate([total[0:1, :], total[2:3, :]], 1) / D
-    square_row = jnp.concatenate([total[1:2, :], total[3:4, :]], 1) / D
-    inv_row = lax.rsqrt(square_row - mean_row * mean_row + EPS)
-    lines = [mean_row, inv_row]
-    for i in range(8):
-        one = s["st"][i * 4 + z] if i < 4 else s["st"][y * 4 + i - 4]
-        lines.append(jnp.concatenate([one[0:1, :], one[2:3, :]], 1) / W - mean_row)
-    lines += [mean_row] * 6
-    s["col"][...] = jnp.concatenate(lines * 8, 0).T
-    rs_b("h2")
+            s[f"d{k}P"][:, i : i + W] = nt(ups, s["dw"][at : at + W, :]).astype(BF)
+
     loads["dw"].wait()
-    down_product(0)
-    rs_a("d0")
-    for cp in wg_cps:
-        cp.wait_recv()
-    rs_zc("h0", (0, 1, 2))
-    rs_b("u0")
-    rs_c("h1", (3, 4, 5))
-    down_product(1)
-    rs_a("d1")
-    rs_b("u1")
-    rs_c("h2", (6, 7, 8))
+    for k in (1, 0):
+        up_product(k)
+        down_product(k)
     own = rows(f * 16, 16)
-    own_inv = s["col"][own, 1:2]
 
     def head_rows(k):
         part = rs_d(f"h{k}") if k else rs_zd("h0")
-        s[f"h{k}G"][own, 0:W] = (part[:, 0:W] * own_inv).astype(BF)
+        s[f"h{k}G"][own, 0:W] = (part[:, 0:W] * s["col"][own, 1:2]).astype(BF)
         s[f"h{k}G"][own, W:512] = part[:, W:512].astype(BF)
         ag_e(f"h{k}")
 
     def up_rows(k):
-        part = rs_d(f"u{k}") * own_inv
+        part = rs_d(f"u{k}") * s["col"][own, 1:2]
         s["rawup"][:, UP[k][0] : UP[k][0] + UP[k][1]] = part
         s[f"a{k}G"][own, :] = gelu_value(part).astype(BF)
         ag_e(f"a{k}")
@@ -438,36 +404,6 @@
         return (
             0.5 * (1.0 + lax.erf(v * 0.7071067811865476)) + v * jnp.exp(-0.5 * v * v) * 0.3989422804014327
         )
-
-    head_rows(0)
-    rs_b("d0")
-    head_rows(1)
-    rs_c("u0", tuple(range(9, 17)))
-    rs_b("d1")
-    head_rows(2)
-    rs_c("u1", tuple(range(17, 21)))
-    ag_f("h0")
-    rs_c("d0")
-    ag_f("h1")
-    rs_c("d1")
-    up_rows(0)
-    ag_f("h2")
-    up_rows(1)
-    ag_h("h0")
-    low_rows(0)
-    ag_h("h1")
-    low_rows(1)
-    ag_f("a0")
-    ag_h("h2")
-    ag_f("a1")
-    ag_i("h0")
-    centred = (inputs - s["col"][:, 0:1]) * s["col"][:, 1:2]
-    s["cen"][...] = centred
-    normed = (centred * gain).astype(BF)
-    s["nrt"][...] = normed.T
-    ag_f("l0")
-    ag_yf("l1")
-    ag_h("a0")
 
     score_scale = HEAD_DIM ** (-0.5)
 
@@ -500,13 +436,73 @@
         s["low"][1, :, lo:hi] = norm_back(tn(ds, q), kn, ks).astype(BF)
         s["low"][2, :, lo:hi] = tn(pl_, da).astype(BF)
 
-    head(0)
+    pl.semaphore_wait(barrier, len(peers))
+    rs_za("h0")
+    rs_a("h2")
+    rs_a("h1")
+    st_cps = [rcopy(stat, stat, dev) for dev in fin_devs]
+    wg_cps = [rcopy(wg, wg, dev) for dev in y_devs] + [rcopy(wz, wz, dev) for dev in z_devs]
+    rs_a("u1")
+    rs_b("h1")
+    rs_b("h2")
+    rs_a("d1")
+    for cp in st_cps:
+        cp.wait_recv()
+    total = sum(s["st"][i] for i in range(16))
+    mean_row = jnp.concatenate([total[0:1, :], total[2:3, :]], 1) / D
+    square_row = jnp.concatenate([total[1:2, :], total[3:4, :]], 1) / D
+    inv_row = lax.rsqrt(square_row - mean_row * mean_row + EPS)
+    lines = [mean_row, inv_row]
+    for i in range(8):
+        one = s["st"][i * 4 + z] if i < 4 else s["st"][y * 4 + i - 4]
+        lines.append(jnp.concatenate([one[0:1, :], one[2:3, :]], 1) / W - mean_row)
+    lines += [mean_row] * 6
+    s["col"][...] = jnp.concatenate(lines * 8, 0).T
+    rs_b("u1")
+    for cp in wg_cps:
+        cp.wait_recv()
+    rs_c("h1", (3, 4, 5))
+    rs_a("u0")
+    rs_c("h2", (6, 7, 8))
+    rs_a("d0")
+    rs_c("u1", tuple(range(15, 21)))
+    rs_b("d1")
+    head_rows(1)
+    rs_b("u0")
+    rs_b("d0")
+    head_rows(2)
+    rs_c("d1")
+    rs_zc("h0", (0, 1, 2))
+    rs_c("u0", tuple(range(9, 15)))
+    ag_f("h1")
+    up_rows(1)
+    ag_f("h2")
+    rs_c("d0")
+    head_rows(0)
+    up_rows(0)
+    low_rows(1)
+    ag_h("h1")
+    ag_h("h2")
+    centred = (inputs - s["col"][:, 0:1]) * s["col"][:, 1:2]
+    s["cen"][...] = centred
+    normed = (centred * gain).astype(BF)
+    s["nrt"][...] = normed.T
+    low_rows(0)
+    ag_f("a1")
+    ag_f("h0")
+    ag_yf("l1")
+    ag_f("a0")
+    ag_f("l0")
     ag_h("a1")
     ag_i("h1")
     head(1)
-    ag_h("l0")
+    ag_h("h0")
+    ag_h("a0")
     ag_i("h2")
     head(2)
+    ag_h("l0")
+    ag_i("h0")
+    head(0)
     ag_i("a0")
     branch = nn(s["att"][...], s["ow"][...]) + nn(s["a0G"][...], s["dw"][0:WIDE, :])
     ag_i("a1")
@@ -534,13 +530,13 @@
     ar_3("n")
     sums = ex_sum(s["fb"], sm_cps)
     sm_cps = ex_start(s["fc"], sums, xh, xh_devs)
-    for i in (0, 512):
-        s["ug_v"][:, i : i + 512] = nn(s["nrt"][...], s["l0G"][:, i : i + 512]).astype(BF)
-    s["ug_v"][:, WIDE:FF] = nn(s["nrt"][...], l1_rows).astype(BF)
+    for i in (0, W):
+        s["ug_v"][:, i : i + W] = nn(s["nrt"][...], s["l0G"][:, i : i + W]).astype(BF)
+        s["ug_v"][:, WIDE + i : WIDE + i + W] = nn(s["nrt"][...], l1_rows[:, i : i + W]).astype(BF)
     ar_4("b")
-    for i in (0, 512):
-        s["dg_v"][i : i + 512, :] = tn(s["a0G"][:, i : i + 512], ups).astype(BF)
-    s["dg_v"][WIDE:FF, :] = tn(s["a1G"][...], ups).astype(BF)
+    for i in (0, W):
+        s["dg_v"][i : i + W, :] = tn(s["a0G"][:, i : i + W], ups).astype(BF)
+        s["dg_v"][WIDE + i : WIDE + i + W, :] = tn(s["a1G"][:, i : i + W], ups).astype(BF)
     s["lo_v"][...] = (s["tok"][...].astype(F32) + ar_5("b")).astype(BF)
     ar_4("n")
     sums = ex_sum(s["fc"], sm_cps)

time: 83.6 us -> 83.1 us (level)
  no operation moved by 1% of the time
where the time goes in v4:
time: 83.1 us; the launch traced here: 83 us
  Pallas kernels  82.3 us (99%)
    pallas_call x1, Pallas kernels, body(): pl.pallas_call(kernel, out_shape=(pltpu.VMEM((T, W), BF), pltpu.VMEM((T,...  80.4 us
    pallas_call x1, Pallas kernels, body(): pl.pallas_call(hand_on, out_shape=tuple((jax.ShapeDtypeStruct(o.shape, o....  1.99 us

profile of v4, /device:TPU:1, one launch (start us, length us, event | category | flops | bytes accessed | tf_op | source)
XLA Modules:
  0.0 83.0 jit_solution(4157128343448047191)
XLA Ops:
  0.6 80.4 %layer.1 = (bf16[256,384]{1,0:T(8,128)(2,1)S(1)}, bf16[256,384]{1,0:T(8,128)(2,1)S(1)}, f32[384]{0:T(512)S(1)}, bf16[3,384,384]{2,1,0:T(8,128)(2,1)S(1)}, bf16[3...) custom-call(bf16[256,384]{1,0:T(8,128)(2,1)} %tok_h.1, f32[384]{0:T(512)} %gain_h.1, ...), custom_call_target="tpu_custom_call" | custom-call | tf_op jit(solution)/shard_map/layer/pallas_call | solution.py:567
  81.0 2.0 %hand_on.1 = (bf16[256,384]{1,0:T(8,128)(2,1)}, bf16[256,384]{1,0:T(8,128)(2,1)}, f32[384]{0:T(512)}, bf16[3,384,384]{2,1,0:T(8,128)(2,1)}, bf16[384,1536]{1,0:T...) custom-call(bf16[256,384]{1,0:T(8,128)(2,1)S(1)} %get-tuple-element.14.refs_0_, ...), custom_call_target="tpu_custom_call" | custom-call | tf_op jit(solution)/shard_map/hand_on/pallas_call | solution.py:591
